TPU v7x, 32 devices: a whole 2x2x4 slice. The times are simulated.
32 devices in a mesh: lon: 8 (over z, x), lat: 4 (over y, core).
Axes of the slice: x: 2, y: 2, z: 4, core: 2. Of those that a mesh axis runs over, the one named last changes fastest.
Arguments:
- ocean_state: float32 [4, 3, 512, 2048], P(None, None, 'lat', 'lon'), may hold values from -6 to 6
- mixing: float32 [3, 512, 2048], P(None, 'lat', 'lon'), may hold values from 0.1 to 1
- land_sea: int32 [512, 2048], P('lat', 'lon'), may hold values 0 or 1
Outputs:
- final_state: float32 [4, 3, 512, 2048], P(None, None, 'lat', 'lon')
All inputs are finite; a program needn't handle non-finite values. No bound on the sum of `land_sea` on one device may be relied on, other than what follows from the above.
Results may differ from a plain program's by a relative error of at most 0.000029.
Values sent between devices are 32-bit elements; how exact they have to be, the bound alone decides.
A program may use at most 128 MiB of HBM per device.

v0:
```python
import functools

import jax
import jax.numpy as jnp
from jax import lax
from jax.experimental import pallas as pl
from jax.experimental.pallas import tpu as pltpu
from jax.sharding import PartitionSpec as P

STEPS = 8
HALO = 2 * STEPS
FIELDS = 4
LEVELS = 3
STATE = FIELDS * LEVELS
PLANES = STATE + LEVELS + 1
SUB = 8
LANE = 128
PER_TILE = LANE // HALO
GROUPS = PLANES // PER_TILE
CHUNK = 4

THERMAL = 0.2
HALINE = 0.15
GRAVITY = 0.5
TIMESTEP = 0.1


def split3(x):
    high = x.astype(jnp.bfloat16)
    rest = x - high.astype(jnp.float32)
    mid = rest.astype(jnp.bfloat16)
    low = (rest - mid.astype(jnp.float32)).astype(jnp.bfloat16)
    return high, mid, low


def flipped(block):
    x, span = block
    rows, cols = x.shape

    def reversal(size, group):
        i = lax.broadcasted_iota(jnp.int32, (size, size), 0)
        j = lax.broadcasted_iota(jnp.int32, (size, size), 1)
        partner = (i // group) * group + (group - 1 - i % group)
        return jnp.where(j == partner, 1.0, 0.0).astype(jnp.bfloat16)

    def dot(a, b):
        return jnp.dot(a, b, preferred_element_type=jnp.float32)

    flip_lanes = reversal(cols, span)
    flip_rows = reversal(rows, HALO)
    high, mid, low = split3(x)
    x = (dot(high, flip_lanes) + dot(mid, flip_lanes)) + dot(low, flip_lanes)
    high, mid, low = split3(x)
    return (dot(flip_rows, high) + dot(flip_rows, mid)) + dot(flip_rows, low)


def exchange_kernel(
    lons, lats, state, mixing, land, north, south, west, east,
    to_west, to_east, to_north, to_south, corner_west, corner_east, send_sem, recv_sem, keep_sem,
):
    rows, cols = land.shape
    ext = rows + 2 * HALO
    lon = lax.axis_index("lon")
    lat = lax.axis_index("lat")
    northmost = lat == lats - 1
    has_south = lat > 0
    left = lax.rem(lon + lons - 1, lons)
    right = lax.rem(lon + 1, lons)
    across = lons - 1 - lon
    across_east = lax.rem(2 * lons - 2 - lon, lons)
    across_west = lax.rem(lons - lon, lons)

    barrier = pltpu.get_barrier_semaphore()

    def greet(x, y):
        pl.semaphore_signal(barrier, inc=1, device_id=(x, y), device_id_type=pl.DeviceIdType.MESH)

    greet(left, lat)
    greet(right, lat)

    @pl.when(has_south)
    def _():
        for x in (left, lon, right):
            greet(x, lat - 1)

    @pl.when(jnp.logical_not(northmost))
    def _():
        for x in (left, lon, right):
            greet(x, lat + 1)

    @pl.when(northmost)
    def _():
        greet(across, lat)

        @pl.when(across_east != lon)
        def _():
            greet(across_east, lat)

        @pl.when(across_west != lon)
        def _():
            greet(across_west, lat)

    def plane(p, row_slice, col_slice):
        if p < STATE:
            return state[p // LEVELS, p % LEVELS, row_slice, col_slice]
        if p < STATE + LEVELS:
            return mixing[p - STATE, row_slice, col_slice]
        return land[row_slice, col_slice].astype(jnp.float32)

    everything = slice(0, cols)
    for p in range(PLANES):
        to_south[p] = plane(p, slice(0, HALO), everything)
        to_north[p] = plane(p, slice(rows - HALO, rows), everything)

    lane = lax.broadcasted_iota(jnp.int32, (rows, LANE), 1)
    for g in range(GROUPS):
        packed_west = jnp.zeros((rows, LANE), jnp.float32)
        packed_east = jnp.zeros((rows, LANE), jnp.float32)
        for slot in range(PER_TILE):
            p = g * PER_TILE + slot
            here = (lane >= slot * HALO) & (lane < (slot + 1) * HALO)
            first = plane(p, slice(0, rows), slice(0, LANE))
            last = plane(p, slice(0, rows), slice(cols - LANE, cols))
            if slot:
                first = pltpu.roll(first, slot * HALO, 1)
            if (slot + 1) * HALO != LANE:
                last = pltpu.roll(last, (slot + 1) * HALO, 1)
            packed_west = jnp.where(here, first, packed_west)
            packed_east = jnp.where(here, last, packed_east)
        to_west[g] = packed_west
        to_east[g] = packed_east

    @pl.when(northmost)
    def _():
        full = to_north[...].reshape(PLANES * HALO, cols)
        index = lax.broadcasted_iota(jnp.int32, full.shape, 0) // HALO
        odd = (index >= 2 * LEVELS) & (index < STATE)
        full = flipped((full, cols))
        to_north[...] = jnp.where(odd, -full, full).reshape(PLANES, HALO, cols)
        shape = (GROUPS * HALO, LANE)
        index = (
            lax.broadcasted_iota(jnp.int32, shape, 0) // HALO * PER_TILE
            + lax.broadcasted_iota(jnp.int32, shape, 1) // HALO
        )
        odd = (index >= 2 * LEVELS) & (index < STATE)
        for source, corner in ((to_west, corner_west), (to_east, corner_east)):
            strip = flipped((source[:, rows - HALO :, :].reshape(shape), HALO))
            corner[...] = jnp.where(odd, -strip, strip).reshape(GROUPS, HALO, LANE)

    @pl.when(jnp.logical_not(northmost))
    def _():
        corner_west[...] = to_west[:, rows - HALO :, :]
        corner_east[...] = to_east[:, rows - HALO :, :]

    @pl.when(has_south & jnp.logical_not(northmost))
    def _():
        pl.semaphore_wait(barrier, 8)

    @pl.when(jnp.logical_not(has_south) & jnp.logical_not(northmost))
    def _():
        pl.semaphore_wait(barrier, 5)

    @pl.when(northmost)
    def _():
        folds = (
            1
            + (across_east != lon).astype(jnp.int32)
            + (across_west != lon).astype(jnp.int32)
        )
        pl.semaphore_wait(barrier, 2 + 3 * has_south.astype(jnp.int32) + folds)

    low = pl.ds(0, HALO)
    high = pl.ds(ext - HALO, HALO)
    middle = pl.ds(HALO, rows)

    def copy(src, dst, send, recv, x, y):
        return pltpu.make_async_remote_copy(
            src_ref=src,
            dst_ref=dst,
            send_sem=send_sem.at[send],
            recv_sem=recv_sem.at[recv],
            device_id=(x, y),
            device_id_type=pl.DeviceIdType.MESH,
        )

    def westward():
        return copy(to_west, east.at[:, middle, :], 0, 1, left, lat)

    def eastward():
        return copy(to_east, west.at[:, middle, :], 1, 0, right, lat)

    def southward():
        return (
            copy(to_south, north, 2, 2, lon, lat - 1),
            copy(to_west.at[:, low, :], east.at[:, high, :], 3, 3, left, lat - 1),
            copy(to_east.at[:, low, :], west.at[:, high, :], 4, 4, right, lat - 1),
        )

    def northward():
        return (
            copy(to_north, south, 5, 5, lon, lat + 1),
            copy(corner_west, east.at[:, low, :], 6, 6, left, lat + 1),
            copy(corner_east, west.at[:, low, :], 7, 7, right, lat + 1),
        )

    def folded():
        return copy(to_north, north, 5, 2, across, lat)

    def folded_east():
        return copy(corner_east, east.at[:, high, :], 6, 3, across_east, lat)

    def folded_west():
        return copy(corner_west, west.at[:, high, :], 7, 4, across_west, lat)

    def kept_east():
        return pltpu.make_async_copy(corner_east, east.at[:, high, :], keep_sem.at[0])

    def kept_west():
        return pltpu.make_async_copy(corner_west, west.at[:, high, :], keep_sem.at[1])

    @pl.when(has_south)
    def _():
        for c in southward():
            c.start()

    @pl.when(jnp.logical_not(northmost))
    def _():
        for c in northward():
            c.start()

    @pl.when(northmost)
    def _():
        folded().start()

        @pl.when(across_east != lon)
        def _():
            folded_east().start()

        @pl.when(across_east == lon)
        def _():
            kept_east().start()

        @pl.when(across_west != lon)
        def _():
            folded_west().start()

        @pl.when(across_west == lon)
        def _():
            kept_west().start()

    westward().start()
    eastward().start()

    @pl.when(jnp.logical_not(has_south))
    def _():
        south[...] = jnp.zeros(south.shape, jnp.float32)
        west[:, 0:HALO, :] = jnp.zeros((GROUPS, HALO, LANE), jnp.float32)
        east[:, 0:HALO, :] = jnp.zeros((GROUPS, HALO, LANE), jnp.float32)

    westward().wait()
    eastward().wait()

    @pl.when(has_south)
    def _():
        for c in southward():
            c.wait_send()
        for c in northward():
            c.wait_recv()

    @pl.when(jnp.logical_not(northmost))
    def _():
        for c in northward():
            c.wait_send()
        for c in southward():
            c.wait_recv()

    @pl.when(northmost)
    def _():
        folded().wait()

        @pl.when(across_east != lon)
        def _():
            folded_east().wait()

        @pl.when(across_east == lon)
        def _():
            kept_east().wait()

        @pl.when(across_west != lon)
        def _():
            folded_west().wait()

        @pl.when(across_west == lon)
        def _():
            kept_west().wait()


def substeps_kernel(
    lons, lats, state, mixing, land, north, south, west, east, out,
    natural, fixed, first, second, mix, wet, spin, sems, out_sem,
):
    rows, cols = land.shape
    ext = rows + 2 * HALO
    depth = ext // SUB
    wide = cols + LANE
    lat = lax.axis_index("lat")
    low, middle, high = pl.ds(0, HALO), pl.ds(HALO, rows), pl.ds(ext - HALO, HALO)

    loads = [
        c
        for t in range(cols // LANE)
        for c in (
            pltpu.make_async_copy(
                state.at[:, :, :, pl.ds(t * LANE, LANE)], natural.at[t, :, :, middle, :], sems.at[2 * t]
            ),
            pltpu.make_async_copy(
                mixing.at[:, :, pl.ds(t * LANE, LANE)],
                fixed.at[t, pl.ds(0, LEVELS), middle, :],
                sems.at[2 * t + 1],
            ),
        )
    ]
    for c in loads:
        c.start()

    r = lax.broadcasted_iota(jnp.int32, (depth, SUB, LANE), 0)
    s = lax.broadcasted_iota(jnp.int32, (depth, SUB, LANE), 1)
    total = rows * lats
    row = lat * rows - HALO + s * depth + r
    row = jnp.where(row >= total, 2 * total - 1 - row, row).astype(jnp.float32)
    turn = jnp.sin(jnp.pi * (row + 0.5) / total - jnp.pi / 2)
    for t in range(wide // LANE):
        spin[:, :, t * LANE : (t + 1) * LANE] = turn

    for t in range(cols // LANE):
        span = slice(t * LANE, (t + 1) * LANE)
        for f in range(FIELDS):
            for k in range(LEVELS):
                natural[t, f, k, 0:HALO, :] = south[f * LEVELS + k, :, span]
                natural[t, f, k, ext - HALO : ext, :] = north[f * LEVELS + k, :, span]
        for p in range(LEVELS + 1):
            fixed[t, p, 0:HALO, :] = south[STATE + p, :, span]
            fixed[t, p, ext - HALO : ext, :] = north[STATE + p, :, span]
        fixed[t, LEVELS, HALO : HALO + rows, :] = land[:, span].astype(jnp.float32)
    for c in loads:
        c.wait()

    lane = lax.broadcasted_iota(jnp.int32, (SUB, LANE), 1)

    def spread(i, carry):
        picked = pl.ds(i, SUB, stride=depth)
        wests = [west[g, picked, :] for g in range(GROUPS)]
        easts = [east[g, picked, :] for g in range(GROUPS)]
        for p in range(PLANES):
            g, slot = p // PER_TILE, p % PER_TILE
            e, w = easts[g], wests[g]
            if slot:
                e = pltpu.roll(e, LANE - slot * HALO, 1)
            if slot != PER_TILE - 1:
                w = pltpu.roll(w, LANE - (slot + 1) * HALO, 1)
            side = jnp.where(lane < HALO, e, jnp.where(lane >= LANE - HALO, w, 0.0))
            for t in range(wide // LANE):
                span = slice(t * LANE, (t + 1) * LANE)
                if t == wide // LANE - 1:
                    value = side
                elif p < STATE:
                    value = natural[t, p // LEVELS, p % LEVELS, picked, :]
                else:
                    value = fixed[t, p - STATE, picked, :]
                if p < STATE:
                    first[p, i + 2, :, span] = value
                elif p < STATE + LEVELS:
                    mix[p - STATE, i, :, span] = value
                else:
                    wet[i, :, span] = TIMESTEP * value
        return carry

    lax.fori_loop(0, depth, spread, 0)

    def ghosts(buf):
        for p in range(STATE):
            for to, source, shift in (
                (0, depth, 1), (1, depth + 1, 1), (depth + 2, 2, SUB - 1), (depth + 3, 3, SUB - 1)
            ):
                buf[p, to] = pltpu.roll(buf[p, source], shift, 0)

    def ahead(x, n):
        return pltpu.roll(x, n % wide, 1)

    def face(before, a, b, after):
        return 7.0 * (a + b) - (before + after)

    def advance(q, new):
        def rows_of(i, carry):
            base = i * CHUNK

            def at(f, k, j):
                return q[f * LEVELS + k, base + j + 2]

            def weights(j):
                total = None
                result = []
                for k in range(LEVELS):
                    density = (
                        (-THERMAL * 0.5 * GRAVITY) * at(0, k, j) + (HALINE * 0.5 * GRAVITY) * at(1, k, j)
                    )
                    total = density if total is None else total + density
                    result.append(total)
                return result

            pressures = {j: weights(j) for j in (-1, 0)}
            below = {}
            for j in range(-1, CHUNK):
                if j >= 0:
                    pressures[j + 1] = weights(j + 1)
                for k in range(LEVELS):
                    fast = (at(3, k, j) + at(3, k, j + 1)) * (1.0 / 24.0)
                    if j >= 0:
                        u = at(2, k, j)
                        along = (u + ahead(u, -1)) * (1.0 / 24.0)
                        m = mix[k, base + j]
                        a = wet[base + j]
                        turn = spin[base + j]
                        pressure = pressures[j][k]
                    for f in range(FIELDS):
                        center, next_row = at(f, k, j), at(f, k, j + 1)
                        prev_row = at(f, k, j - 1)
                        upper = fast * face(prev_row, center, next_row, at(f, k, j + 2))
                        lower = below.get((f, k))
                        below[f, k] = upper
                        if j < 0:
                            continue
                        east_1, west_1, east_2 = ahead(center, -1), ahead(center, 1), ahead(center, -2)
                        flux = along * face(west_1, center, east_1, east_2)
                        advection = (flux - ahead(flux, 1)) + (upper - lower)
                        around = (east_1 + west_1) + (next_row + prev_row)
                        if f < 2:
                            if k == 0:
                                mixed = around + (0.5 * at(f, 1, j) - 4.5 * center)
                            elif k == LEVELS - 1:
                                mixed = around + (0.5 * at(f, k - 1, j) - 4.5 * center)
                            else:
                                mixed = around + (0.5 * (at(f, k - 1, j) + at(f, k + 1, j)) - 5.0 * center)
                        else:
                            mixed = around - 4.0 * center
                        tendency = m * mixed - advection
                        if f == 2:
                            slope = ahead(pressure, -1) - ahead(pressure, 1)
                            tendency = tendency + (turn * at(3, k, j) - slope)
                        elif f == 3:
                            slope = pressures[j + 1][k] - pressures[j - 1][k]
                            tendency = tendency - (turn * at(2, k, j) + slope)
                        new[f * LEVELS + k, base + j + 2] = center + a * tendency
            return carry

        lax.fori_loop(0, depth // CHUNK, rows_of, 0)

    def pair(i, carry):
        ghosts(first)
        advance(first, second)
        ghosts(second)
        advance(second, first)
        return carry

    lax.fori_loop(0, STEPS // 2, pair, 0)

    def gather(i, carry):
        for p in range(STATE):
            for t in range(cols // LANE):
                span = slice(t * LANE, (t + 1) * LANE)
                natural[t, p // LEVELS, p % LEVELS, pl.ds(i, SUB, stride=depth), :] = first[p, i + 2, :, span]
        return carry

    lax.fori_loop(0, depth, gather, 0)
    stores = [
        pltpu.make_async_copy(
            natural.at[t, :, :, middle, :], out.at[:, :, :, pl.ds(t * LANE, LANE)], out_sem.at[t]
        )
        for t in range(cols // LANE)
    ]
    for c in stores:
        c.start()
    for c in stores:
        c.wait()


def body(lons, lats, ocean_state, mixing, land_sea):
    rows, cols = land_sea.shape
    ext, wide = rows + 2 * HALO, cols + LANE
    depth = ext // SUB
    f32 = jnp.float32
    vmem = pl.BlockSpec(memory_space=pltpu.VMEM)
    hbm = pl.BlockSpec(memory_space=pl.ANY)
    halos = pl.pallas_call(
        functools.partial(exchange_kernel, lons, lats),
        out_shape=[
            jax.ShapeDtypeStruct((PLANES, HALO, cols), f32),
            jax.ShapeDtypeStruct((PLANES, HALO, cols), f32),
            jax.ShapeDtypeStruct((GROUPS, ext, LANE), f32),
            jax.ShapeDtypeStruct((GROUPS, ext, LANE), f32),
        ],
        in_specs=[vmem] * 3,
        out_specs=[vmem] * 4,
        scratch_shapes=[
            pltpu.VMEM((GROUPS, rows, LANE), f32),
            pltpu.VMEM((GROUPS, rows, LANE), f32),
            pltpu.VMEM((PLANES, HALO, cols), f32),
            pltpu.VMEM((PLANES, HALO, cols), f32),
            pltpu.VMEM((GROUPS, HALO, LANE), f32),
            pltpu.VMEM((GROUPS, HALO, LANE), f32),
            pltpu.SemaphoreType.DMA((8,)),
            pltpu.SemaphoreType.DMA((8,)),
            pltpu.SemaphoreType.DMA((2,)),
        ],
        compiler_params=pltpu.CompilerParams(
            collective_id=0, has_side_effects=True, vmem_limit_bytes=32 * 2**20
        ),
        name="exchange",
    )(ocean_state, mixing, land_sea)
    return pl.pallas_call(
        functools.partial(substeps_kernel, lons, lats),
        out_shape=jax.ShapeDtypeStruct(ocean_state.shape, f32),
        in_specs=[hbm, hbm] + [vmem] * 5,
        out_specs=hbm,
        scratch_shapes=[
            pltpu.VMEM((cols // LANE, FIELDS, LEVELS, ext, LANE), f32),
            pltpu.VMEM((cols // LANE, LEVELS + 1, ext, LANE), f32),
            pltpu.VMEM((STATE, depth + 4, SUB, wide), f32),
            pltpu.VMEM((STATE, depth + 4, SUB, wide), f32),
            pltpu.VMEM((LEVELS, depth, SUB, wide), f32),
            pltpu.VMEM((depth, SUB, wide), f32),
            pltpu.VMEM((depth, SUB, wide), f32),
            pltpu.SemaphoreType.DMA((2 * (cols // LANE),)),
            pltpu.SemaphoreType.DMA((cols // LANE,)),
        ],
        compiler_params=pltpu.CompilerParams(vmem_limit_bytes=48 * 2**20),
        name="substeps",
    )(ocean_state, mixing, land_sea, *halos)


def solution(mesh):
    in_specs = (P(None, None, "lat", "lon"), P(None, "lat", "lon"), P("lat", "lon"))
    out_specs = P(None, None, "lat", "lon")
    run = functools.partial(body, mesh.shape["lon"], mesh.shape["lat"])
    return jax.shard_map(run, mesh=mesh, in_specs=in_specs, out_specs=out_specs, check_vma=False)
```

profile of v0, /device:TPU:7, one launch (start us, length us, event | category | flops | bytes accessed | tf_op | source)
XLA Modules:
  0.0 163.3 jit_solution(10774321580546759547)
XLA Ops:
  0.0 0.0 copy-start
  0.0 1.4 copy-done
  1.4 0.0 copy-start.2
  1.4 1.0 copy-done.2
  2.4 0.0 copy-start.4
  2.4 0.9 copy-done.4
  3.3 0.0 copy-start.1
  3.3 0.0 copy-start.3
  3.3 0.0 copy-start.5
  3.3 14.6 %exchange.1 = (f32[16,16,256]{2,1,0:T(8,128)S(1)}, f32[16,16,256]{2,1,0:T(8,128)S(1)}, f32[2,160,128]{2,1,0:T(8,128)S(1)}, f32[2,160,128]{2,1,0:T(8,128)S(1)}) custom-call(f32[4,3,128,256]{3,2,1,0:T(8,128)S(1)} %copy-done, f32[3,128,256]{2,1,0:T(8,128)S(1)} %copy-done.2, s32[128,256]{1,0:T(8,128)S(1)} %copy-done.4), custom_call_target="tpu_custom_call" | custom-call | tf_op jit(solution)/shard_map/exchange/pallas_call | solution.py:494
  17.9 0.0 copy-done.1
  17.9 0.0 copy-done.3
  17.9 0.0 copy-done.5
  17.9 145.3 %substeps.1 = f32[4,3,128,256]{3,2,1,0:T(8,128)} custom-call(f32[4,3,128,256]{3,2,1,0:T(8,128)S(1)} %copy-done.1, f32[3,128,256]{2,1,0:T(8,128)S(1)} %copy-done.3, s32[128,256]{1,0:T(8,128)S(1)} %copy-done.5, f32[16,16,256]{2,1,0:T(8,128)S(1)} %get-tuple-element.9.north, f32[16,16,256]{2,1,0:T(8,128)S(1)} %get-tuple-element.10.south, ...), custom_call_target="tpu_custom_call" | custom-call | tf_op jit(solution)/shard_map/substeps/pallas_call | solution.py:520
Async XLA Ops:
  0.0 1.4 copy-start
  1.4 1.0 copy-start.2
  2.4 0.9 copy-start.4
  3.3 14.6 %copy-start.1 = (f32[4,3,128,256]{3,2,1,0:T(8,128)S(1)}, f32[4,3,128,256]{3,2,1,0:T(8,128)}, u32[]{:S(2)}) copy-start(f32[4,3,128,256]{3,2,1,0:T(8,128)} %state.3) | copy-start | bytes 4718596
  3.3 14.6 %copy-start.3 = (f32[3,128,256]{2,1,0:T(8,128)S(1)}, f32[3,128,256]{2,1,0:T(8,128)}, u32[]{:S(2)}) copy-start(f32[3,128,256]{2,1,0:T(8,128)} %mixing.3) | copy-start | bytes 1179652
  3.3 14.6 %copy-start.5 = (s32[128,256]{1,0:T(8,128)S(1)}, s32[128,256]{1,0:T(8,128)}, u32[]{:S(2)}) copy-start(s32[128,256]{1,0:T(8,128)} %land.3) | copy-start | bytes 393220
where the time goes:
time: 163 us
  Pallas kernels  160 us (98%)
  local copies, waits for them, and re-layouts  3.32 us (2%)
    pallas_call x1, Pallas kernels, body(): pl.pallas_call(functools.partial(substeps_kernel, lons, lats), out_shape=...  145 us
    pallas_call x1, Pallas kernels, body(): pl.pallas_call(functools.partial(exchange_kernel, lons, lats), out_shape=...  14.6 us
    unnamed x12, local copies, waits for them, and re-layouts  3.32 us

commit v1 on v0

--- a/solution.py
+++ b/solution.py
@@ -17,7 +17,8 @@
 LANE = 128
 PER_TILE = LANE // HALO
 GROUPS = PLANES // PER_TILE
-CHUNK = 4
+SIDE = 2
+HALF = LANE // SIDE
 
 THERMAL = 0.2
 HALINE = 0.15
@@ -295,16 +296,25 @@
             kept_west().wait()
 
 
+def exact_dot(x, selection):
+    high, mid, low = split3(x)
+
+    def dot(a):
+        return jnp.dot(a, selection, preferred_element_type=jnp.float32)
+
+    return (dot(high) + dot(mid)) + dot(low)
+
+
 def substeps_kernel(
     lons, lats, state, mixing, land, north, south, west, east, out,
-    natural, fixed, first, second, mix, wet, spin, sems, out_sem,
+    natural, fixed, joined, first, second, mix, spin, fast, along, press, to_tiles, from_tiles, sems, out_sem,
 ):
     rows, cols = land.shape
     ext = rows + 2 * HALO
-    depth = ext // SUB
-    wide = cols + LANE
+    depth = spin.shape[0]
+    tiles = first.shape[2]
     lat = lax.axis_index("lat")
-    low, middle, high = pl.ds(0, HALO), pl.ds(HALO, rows), pl.ds(ext - HALO, HALO)
+    middle = pl.ds(HALO, rows)
 
     loads = [
         c
@@ -323,14 +333,23 @@
     for c in loads:
         c.start()
 
+    def selection(shape, tile_dim):
+        j = lax.broadcasted_iota(jnp.int32, shape, tile_dim)
+        n = lax.broadcasted_iota(jnp.int32, shape, 1 - tile_dim)
+        home = tiles * (j & (HALF - 1)) + j // HALF - HALO
+        home = jnp.where(home < 0, home + tiles * HALF, home)
+        return jnp.where((n == home) & (j < tiles * HALF), 1.0, 0.0).astype(jnp.bfloat16)
+
+    to_tiles[...] = selection(to_tiles.shape, 1)
+    from_tiles[...] = selection(from_tiles.shape, 0)
+
     r = lax.broadcasted_iota(jnp.int32, (depth, SUB, LANE), 0)
     s = lax.broadcasted_iota(jnp.int32, (depth, SUB, LANE), 1)
+    h = lax.broadcasted_iota(jnp.int32, (depth, SUB, LANE), 2) // HALF
     total = rows * lats
-    row = lat * rows - HALO + s * depth + r
+    row = lat * rows - HALO + (SIDE * s + h) * depth + r
     row = jnp.where(row >= total, 2 * total - 1 - row, row).astype(jnp.float32)
-    turn = jnp.sin(jnp.pi * (row + 0.5) / total - jnp.pi / 2)
-    for t in range(wide // LANE):
-        spin[:, :, t * LANE : (t + 1) * LANE] = turn
+    spin[...] = jnp.sin(jnp.pi * (row + 0.5) / total - jnp.pi / 2)
 
     for t in range(cols // LANE):
         span = slice(t * LANE, (t + 1) * LANE)
@@ -346,132 +365,208 @@
         c.wait()
 
     lane = lax.broadcasted_iota(jnp.int32, (SUB, LANE), 1)
-
-    def spread(i, carry):
-        picked = pl.ds(i, SUB, stride=depth)
-        wests = [west[g, picked, :] for g in range(GROUPS)]
-        easts = [east[g, picked, :] for g in range(GROUPS)]
-        for p in range(PLANES):
-            g, slot = p // PER_TILE, p % PER_TILE
-            e, w = easts[g], wests[g]
-            if slot:
-                e = pltpu.roll(e, LANE - slot * HALO, 1)
-            if slot != PER_TILE - 1:
-                w = pltpu.roll(w, LANE - (slot + 1) * HALO, 1)
-            side = jnp.where(lane < HALO, e, jnp.where(lane >= LANE - HALO, w, 0.0))
-            for t in range(wide // LANE):
-                span = slice(t * LANE, (t + 1) * LANE)
-                if t == wide // LANE - 1:
-                    value = side
-                elif p < STATE:
-                    value = natural[t, p // LEVELS, p % LEVELS, picked, :]
-                else:
-                    value = fixed[t, p - STATE, picked, :]
-                if p < STATE:
-                    first[p, i + 2, :, span] = value
-                elif p < STATE + LEVELS:
-                    mix[p - STATE, i, :, span] = value
-                else:
-                    wet[i, :, span] = TIMESTEP * value
+    lower_half = lane < HALF
+    west_at = tiles * HALF - cols - HALO
+
+    def join(i, carry):
+        for h in range(SIDE):
+            picked = pl.ds(h * depth + i, SUB, stride=SIDE * depth)
+            for g in range(GROUPS):
+                e_all, w_all = east[g, picked, :], west[g, picked, :]
+                for slot in range(PER_TILE):
+                    p = g * PER_TILE + slot
+                    e, w = e_all, w_all
+                    if slot:
+                        e = pltpu.roll(e, LANE - slot * HALO, 1)
+                    if (west_at - slot * HALO) % LANE:
+                        w = pltpu.roll(w, (west_at - slot * HALO) % LANE, 1)
+                    side = jnp.where(
+                        lane < HALO, e, jnp.where((lane >= west_at) & (lane < west_at + HALO), w, 0.0)
+                    )
+                    for t in range(cols // LANE):
+                        if p < STATE:
+                            value = natural[t, p // LEVELS, p % LEVELS, picked, :]
+                        else:
+                            value = fixed[t, p - STATE, picked, :]
+                        joined[p, h, i, :, t * LANE : (t + 1) * LANE] = value
+                    joined[p, h, i, :, cols : cols + LANE] = side
         return carry
 
-    lax.fori_loop(0, depth, spread, 0)
+    lax.fori_loop(0, depth, join, 0)
+
+    half_rows = depth * SUB
+    wide = cols + LANE
+    low_lanes = lax.broadcasted_iota(jnp.int32, (half_rows, LANE), 1) < HALF
+
+    def tiled(p):
+        halves = []
+        for h in range(SIDE):
+            halves.append(exact_dot(joined[p, h].reshape(half_rows, wide), to_tiles[...]))
+        result = []
+        for c in range(tiles):
+            span = slice(c // 2 * LANE, (c // 2 + 1) * LANE)
+            a, b = halves[0][:, span], halves[1][:, span]
+            if c % 2:
+                a = pltpu.roll(a, HALF, 1)
+            else:
+                b = pltpu.roll(b, HALF, 1)
+            result.append(jnp.where(low_lanes, a, b).reshape(depth, SUB, LANE))
+        return result
+
+    def place(p, carry):
+        for c, value in enumerate(tiled(p)):
+            first[p, 2 : depth + 2, c] = value
+        return carry
+
+    lax.fori_loop(0, STATE, place, 0)
+
+    def place_fixed(p, carry):
+        for c, value in enumerate(tiled(STATE + p)):
+            mix[p, :, c] = value
+        return carry
+
+    lax.fori_loop(0, LEVELS + 1, place_fixed, 0)
 
     def ghosts(buf):
-        for p in range(STATE):
-            for to, source, shift in (
-                (0, depth, 1), (1, depth + 1, 1), (depth + 2, 2, SUB - 1), (depth + 3, 3, SUB - 1)
-            ):
-                buf[p, to] = pltpu.roll(buf[p, source], shift, 0)
-
-    def ahead(x, n):
-        return pltpu.roll(x, n % wide, 1)
+        def one(p, carry):
+            for c in range(tiles):
+                for to, source, ahead in ((0, depth, 0), (1, depth + 1, 0), (depth + 2, 2, 1), (depth + 3, 3, 1)):
+                    x = pltpu.roll(buf[p, source, c], HALF, 1)
+                    if ahead:
+                        buf[p, to, c] = jnp.where(lower_half, x, pltpu.roll(x, SUB - 1, 0))
+                    else:
+                        buf[p, to, c] = jnp.where(lower_half, pltpu.roll(x, 1, 0), x)
+            return carry
+
+        lax.fori_loop(0, STATE, one, 0)
+
+    def back(x):
+        return pltpu.roll(x, 1, 1)
+
+    def ahead(x):
+        return pltpu.roll(x, LANE - 1, 1)
 
     def face(before, a, b, after):
         return 7.0 * (a + b) - (before + after)
 
+    def prepare(q):
+        def weights(j, carry):
+            for c in range(tiles):
+                running = None
+                for k in range(LEVELS):
+                    density = (
+                        (-THERMAL * 0.5 * GRAVITY) * q[k, j + 1, c]
+                        + (HALINE * 0.5 * GRAVITY) * q[LEVELS + k, j + 1, c]
+                    )
+                    running = density if running is None else running + density
+                    press[k, j, c] = running
+            return carry
+
+        lax.fori_loop(0, depth + 2, weights, 0)
+
+        def speeds(j, carry):
+            for k in range(LEVELS):
+                for c in range(tiles):
+                    v = 3 * LEVELS + k
+                    fast[k, j, c] = (q[v, j + 1, c] + q[v, j + 2, c]) * (1.0 / 24.0)
+                u = [q[2 * LEVELS + k, j + 1, c] for c in range(tiles)]
+                u.append(ahead(u[0]))
+                for c in range(tiles):
+                    along[k, j, c] = (u[c] + u[c + 1]) * (1.0 / 24.0)
+            return carry
+
+        lax.fori_loop(0, depth + 1, speeds, 0)
+
+    chunk = depth // 2
+    each = range(tiles)
+
     def advance(q, new):
         def rows_of(i, carry):
-            base = i * CHUNK
-
-            def at(f, k, j):
-                return q[f * LEVELS + k, base + j + 2]
-
-            def weights(j):
-                total = None
-                result = []
-                for k in range(LEVELS):
-                    density = (
-                        (-THERMAL * 0.5 * GRAVITY) * at(0, k, j) + (HALINE * 0.5 * GRAVITY) * at(1, k, j)
-                    )
-                    total = density if total is None else total + density
-                    result.append(total)
-                return result
-
-            pressures = {j: weights(j) for j in (-1, 0)}
-            below = {}
-            for j in range(-1, CHUNK):
-                if j >= 0:
-                    pressures[j + 1] = weights(j + 1)
-                for k in range(LEVELS):
-                    fast = (at(3, k, j) + at(3, k, j + 1)) * (1.0 / 24.0)
-                    if j >= 0:
-                        u = at(2, k, j)
-                        along = (u + ahead(u, -1)) * (1.0 / 24.0)
-                        m = mix[k, base + j]
-                        a = wet[base + j]
-                        turn = spin[base + j]
-                        pressure = pressures[j][k]
-                    for f in range(FIELDS):
-                        center, next_row = at(f, k, j), at(f, k, j + 1)
-                        prev_row = at(f, k, j - 1)
-                        upper = fast * face(prev_row, center, next_row, at(f, k, j + 2))
-                        lower = below.get((f, k))
-                        below[f, k] = upper
+            base = i * chunk
+            for k in range(LEVELS):
+                for f in range(FIELDS):
+                    p = f * LEVELS + k
+
+                    def line(j, p=p):
+                        return [q[p, base + j + 2, c] for c in each]
+
+                    lines = {j: line(j) for j in (-2, -1, 0)}
+                    lower = None
+                    for j in range(-1, chunk):
+                        lines[j + 2] = line(j + 2)
+                        prev, here, succ, succ2 = (lines[j + d] for d in (-1, 0, 1, 2))
+                        upper = [
+                            fast[k, base + j + 1, c] * face(prev[c], here[c], succ[c], succ2[c]) for c in each
+                        ]
                         if j < 0:
+                            lower = upper
                             continue
-                        east_1, west_1, east_2 = ahead(center, -1), ahead(center, 1), ahead(center, -2)
-                        flux = along * face(west_1, center, east_1, east_2)
-                        advection = (flux - ahead(flux, 1)) + (upper - lower)
-                        around = (east_1 + west_1) + (next_row + prev_row)
-                        if f < 2:
-                            if k == 0:
-                                mixed = around + (0.5 * at(f, 1, j) - 4.5 * center)
-                            elif k == LEVELS - 1:
-                                mixed = around + (0.5 * at(f, k - 1, j) - 4.5 * center)
+                        ring = [back(here[-1])] + here + [ahead(here[0]), ahead(here[1])]
+                        flux = [
+                            along[k, base + j + 1, c] * face(ring[c], ring[c + 1], ring[c + 2], ring[c + 3])
+                            for c in each
+                        ]
+                        flux = [back(flux[-1])] + flux
+                        if f == 2:
+                            load = [press[k, base + j + 1, c] for c in each]
+                            load = [back(load[-1])] + load + [ahead(load[0])]
+                        for c in each:
+                            center = here[c]
+                            advection = (flux[c + 1] - flux[c]) + (upper[c] - lower[c])
+                            around = (ring[c] + ring[c + 2]) + (prev[c] + succ[c])
+                            if f < 2:
+                                if k == 0 or k == LEVELS - 1:
+                                    other = q[p + (1 if k == 0 else -1), base + j + 2, c]
+                                    mixed = around + (0.5 * other - 4.5 * center)
+                                else:
+                                    others = q[p - 1, base + j + 2, c] + q[p + 1, base + j + 2, c]
+                                    mixed = around + (0.5 * others - 5.0 * center)
                             else:
-                                mixed = around + (0.5 * (at(f, k - 1, j) + at(f, k + 1, j)) - 5.0 * center)
-                        else:
-                            mixed = around - 4.0 * center
-                        tendency = m * mixed - advection
-                        if f == 2:
-                            slope = ahead(pressure, -1) - ahead(pressure, 1)
-                            tendency = tendency + (turn * at(3, k, j) - slope)
-                        elif f == 3:
-                            slope = pressures[j + 1][k] - pressures[j - 1][k]
-                            tendency = tendency - (turn * at(2, k, j) + slope)
-                        new[f * LEVELS + k, base + j + 2] = center + a * tendency
+                                mixed = around - 4.0 * center
+                            tendency = mix[k, base + j, c] * mixed - advection
+                            if f == 2:
+                                turned = spin[base + j] * q[p + LEVELS, base + j + 2, c]
+                                tendency = tendency + (turned - (load[c + 2] - load[c]))
+                            elif f == 3:
+                                turned = spin[base + j] * q[p - LEVELS, base + j + 2, c]
+                                slope = press[k, base + j + 2, c] - press[k, base + j, c]
+                                tendency = tendency - (turned + slope)
+                            wet = TIMESTEP * mix[LEVELS, base + j, c]
+                            new[p, base + j + 2, c] = center + wet * tendency
+                        lower = upper
             return carry
 
-        lax.fori_loop(0, depth // CHUNK, rows_of, 0)
+        lax.fori_loop(0, depth // chunk, rows_of, 0)
 
     def pair(i, carry):
-        ghosts(first)
-        advance(first, second)
-        ghosts(second)
-        advance(second, first)
+        for q, new in ((first, second), (second, first)):
+            ghosts(q)
+            prepare(q)
+            advance(q, new)
         return carry
 
     lax.fori_loop(0, STEPS // 2, pair, 0)
 
-    def gather(i, carry):
-        for p in range(STATE):
-            for t in range(cols // LANE):
-                span = slice(t * LANE, (t + 1) * LANE)
-                natural[t, p // LEVELS, p % LEVELS, pl.ds(i, SUB, stride=depth), :] = first[p, i + 2, :, span]
+    def gather(p, carry):
+        value = [first[p, 2 : depth + 2, c].reshape(half_rows, LANE) for c in each]
+        for h in range(SIDE):
+            parts = []
+            for c in range(0, tiles, 2):
+                a = value[c] if h == 0 else pltpu.roll(value[c], HALF, 1)
+                if c + 1 < tiles:
+                    b = value[c + 1] if h == 1 else pltpu.roll(value[c + 1], HALF, 1)
+                else:
+                    b = jnp.zeros_like(a)
+                parts.append(jnp.where(low_lanes, a, b))
+            flat = exact_dot(jnp.concatenate(parts, axis=1), from_tiles[...])
+            for i in range(depth):
+                for t in range(cols // LANE):
+                    natural[t, p // LEVELS, p % LEVELS, pl.ds(h * depth + i, SUB, stride=SIDE * depth), :] = flat[
+                        i * SUB : (i + 1) * SUB, t * LANE : (t + 1) * LANE
+                    ]
         return carry
 
-    lax.fori_loop(0, depth, gather, 0)
+    lax.fori_loop(0, STATE, gather, 0)
     stores = [
         pltpu.make_async_copy(
             natural.at[t, :, :, middle, :], out.at[:, :, :, pl.ds(t * LANE, LANE)], out_sem.at[t]
@@ -487,7 +582,8 @@
 def body(lons, lats, ocean_state, mixing, land_sea):
     rows, cols = land_sea.shape
     ext, wide = rows + 2 * HALO, cols + LANE
-    depth = ext // SUB
+    depth = ext // (SUB * SIDE)
+    tiles = -(-(cols + 2 * HALO) // HALF)
     f32 = jnp.float32
     vmem = pl.BlockSpec(memory_space=pltpu.VMEM)
     hbm = pl.BlockSpec(memory_space=pl.ANY)
@@ -525,11 +621,16 @@
         scratch_shapes=[
             pltpu.VMEM((cols // LANE, FIELDS, LEVELS, ext, LANE), f32),
             pltpu.VMEM((cols // LANE, LEVELS + 1, ext, LANE), f32),
-            pltpu.VMEM((STATE, depth + 4, SUB, wide), f32),
-            pltpu.VMEM((STATE, depth + 4, SUB, wide), f32),
-            pltpu.VMEM((LEVELS, depth, SUB, wide), f32),
-            pltpu.VMEM((depth, SUB, wide), f32),
-            pltpu.VMEM((depth, SUB, wide), f32),
+            pltpu.VMEM((PLANES, SIDE, depth, SUB, wide), f32),
+            pltpu.VMEM((STATE, depth + 4, tiles, SUB, LANE), f32),
+            pltpu.VMEM((STATE, depth + 4, tiles, SUB, LANE), f32),
+            pltpu.VMEM((LEVELS + 1, depth, tiles, SUB, LANE), f32),
+            pltpu.VMEM((depth, SUB, LANE), f32),
+            pltpu.VMEM((LEVELS, depth + 1, tiles, SUB, LANE), f32),
+            pltpu.VMEM((LEVELS, depth + 1, tiles, SUB, LANE), f32),
+            pltpu.VMEM((LEVELS, depth + 2, tiles, SUB, LANE), f32),
+            pltpu.VMEM((wide, wide), jnp.bfloat16),
+            pltpu.VMEM((wide, cols), jnp.bfloat16),
             pltpu.SemaphoreType.DMA((2 * (cols // LANE),)),
             pltpu.SemaphoreType.DMA((cols // LANE,)),
         ],

time: 163 us -> 93.1 us (0.57)
  Pallas kernels: 160 us -> 89.6 us
    pallas_call x1, Pallas kernels: 145 us -> 75 us  [body(): pl.pallas_call(functools.partial(substeps_kernel, lons, lats), out_shape=...]
where the time goes in v1:
time: 93.1 us; the launch traced here: 92.9 us
  Pallas kernels  89.6 us (96%)
  local copies, waits for them, and re-layouts  3.32 us (4%)
    pallas_call x1, Pallas kernels, body(): pl.pallas_call(functools.partial(substeps_kernel, lons, lats), out_shape=...  75 us
    pallas_call x1, Pallas kernels, body(): pl.pallas_call(functools.partial(exchange_kernel, lons, lats), out_shape=...  14.6 us
    unnamed x12, local copies, waits for them, and re-layouts  3.32 us

profile of v1, /device:TPU:7, one launch (start us, length us, event | category | flops | bytes accessed | tf_op | source)
XLA Modules:
  0.0 92.9 jit_solution(5838691248030001434)
XLA Ops:
  0.0 0.0 copy-start
  0.0 1.4 %copy-done = f32[4,3,128,256]{3,2,1,0:T(8,128)S(1)} copy-done((f32[4,3,128,256]{3,2,1,0:T(8,128)S(1)}, f32[4,3,128,256]{3,2,1,0:T(8,128)}, u32[]{:S(2)}) %copy-start) | copy-done | bytes 1572888
  1.4 0.0 copy-start.2
  1.4 1.0 %copy-done.2 = f32[3,128,256]{2,1,0:T(8,128)S(1)} copy-done((f32[3,128,256]{2,1,0:T(8,128)S(1)}, f32[3,128,256]{2,1,0:T(8,128)}, u32[]{:S(2)}) %copy-start.2) | copy-done | bytes 393240
  2.4 0.0 copy-start.4
  2.4 0.9 copy-done.4
  3.3 0.0 copy-start.1
  3.3 0.0 copy-start.3
  3.3 0.0 copy-start.5
  3.3 14.6 %exchange.1 = (f32[16,16,256]{2,1,0:T(8,128)S(1)}, f32[16,16,256]{2,1,0:T(8,128)S(1)}, f32[2,160,128]{2,1,0:T(8,128)S(1)}, f32[2,160,128]{2,1,0:T(8,128)S(1)}) custom-call(f32[4,3,128,256]{3,2,1,0:T(8,128)S(1)} %copy-done, f32[3,128,256]{2,1,0:T(8,128)S(1)} %copy-done.2, s32[128,256]{1,0:T(8,128)S(1)} %copy-done.4), custom_call_target="tpu_custom_call" | custom-call | tf_op jit(solution)/shard_map/exchange/pallas_call | solution.py:590
  17.9 0.0 copy-done.1
  17.9 0.0 copy-done.3
  17.9 0.0 copy-done.5
  17.9 75.0 %substeps.1 = f32[4,3,128,256]{3,2,1,0:T(8,128)} custom-call(f32[4,3,128,256]{3,2,1,0:T(8,128)S(1)} %copy-done.1, f32[3,128,256]{2,1,0:T(8,128)S(1)} %copy-done.3, s32[128,256]{1,0:T(8,128)S(1)} %copy-done.5, f32[16,16,256]{2,1,0:T(8,128)S(1)} %get-tuple-element.9.north, f32[16,16,256]{2,1,0:T(8,128)S(1)} %get-tuple-element.10.south, ...), custom_call_target="tpu_custom_call" | custom-call | tf_op jit(solution)/shard_map/substeps/pallas_call | solution.py:616
Async XLA Ops:
  0.0 1.4 %copy-start = (f32[4,3,128,256]{3,2,1,0:T(8,128)S(1)}, f32[4,3,128,256]{3,2,1,0:T(8,128)}, u32[]{:S(2)}) copy-start(f32[4,3,128,256]{3,2,1,0:T(8,128)} %state.3) | copy-start | bytes 4718596
  1.4 1.0 %copy-start.2 = (f32[3,128,256]{2,1,0:T(8,128)S(1)}, f32[3,128,256]{2,1,0:T(8,128)}, u32[]{:S(2)}) copy-start(f32[3,128,256]{2,1,0:T(8,128)} %mixing.3) | copy-start | bytes 1179652
  2.4 0.9 copy-start.4
  3.3 14.6 %copy-start.1 = (f32[4,3,128,256]{3,2,1,0:T(8,128)S(1)}, f32[4,3,128,256]{3,2,1,0:T(8,128)}, u32[]{:S(2)}) copy-start(f32[4,3,128,256]{3,2,1,0:T(8,128)} %state.3) | copy-start | bytes 4718596
  3.3 14.6 %copy-start.3 = (f32[3,128,256]{2,1,0:T(8,128)S(1)}, f32[3,128,256]{2,1,0:T(8,128)}, u32[]{:S(2)}) copy-start(f32[3,128,256]{2,1,0:T(8,128)} %mixing.3) | copy-start | bytes 1179652
  3.3 14.6 %copy-start.5 = (s32[128,256]{1,0:T(8,128)S(1)}, s32[128,256]{1,0:T(8,128)}, u32[]{:S(2)}) copy-start(s32[128,256]{1,0:T(8,128)} %land.3) | copy-start | bytes 393220

commit v2 on v1

--- a/solution.py
+++ b/solution.py
@@ -297,12 +297,10 @@
 
 
 def exact_dot(x, selection):
-    high, mid, low = split3(x)
-
-    def dot(a):
-        return jnp.dot(a, selection, preferred_element_type=jnp.float32)
-
-    return (dot(high) + dot(mid)) + dot(low)
+    rows = x.shape[0]
+    pieces = jnp.concatenate(split3(x), axis=0)
+    y = jnp.dot(pieces, selection, preferred_element_type=jnp.float32)
+    return (y[:rows] + y[rows : 2 * rows]) + y[2 * rows :]
 
 
 def substeps_kernel(
@@ -312,7 +310,7 @@
     rows, cols = land.shape
     ext = rows + 2 * HALO
     depth = spin.shape[0]
-    tiles = first.shape[2]
+    tiles = mix.shape[2]
     lat = lax.axis_index("lat")
     middle = pl.ds(HALO, rows)
 
@@ -398,157 +396,146 @@
     wide = cols + LANE
     low_lanes = lax.broadcasted_iota(jnp.int32, (half_rows, LANE), 1) < HALF
 
+    each = range(tiles)
+    edge = 2
+
+    def back(x):
+        return pltpu.roll(x, 1, 1)
+
+    def ahead(x):
+        return pltpu.roll(x, LANE - 1, 1)
+
+    def publish(buf, p, j, row):
+        for c in each:
+            buf[p, j + 2, c + edge] = row[c]
+        buf[p, j + 2, 0] = back(row[-2])
+        buf[p, j + 2, 1] = back(row[-1])
+        buf[p, j + 2, tiles + edge] = ahead(row[0])
+        buf[p, j + 2, tiles + edge + 1] = ahead(row[1])
+        if j < 2:
+            for c in each:
+                x = pltpu.roll(row[c], HALF, 1)
+                buf[p, depth + 2 + j, c + edge] = jnp.where(lower_half, x, pltpu.roll(x, SUB - 1, 0))
+        if j >= depth - 2:
+            for c in each:
+                x = pltpu.roll(row[c], HALF, 1)
+                buf[p, j + 2 - depth, c + edge] = jnp.where(lower_half, pltpu.roll(x, 1, 0), x)
+
     def tiled(p):
-        halves = []
-        for h in range(SIDE):
-            halves.append(exact_dot(joined[p, h].reshape(half_rows, wide), to_tiles[...]))
+        both = exact_dot(joined[p].reshape(SIDE * half_rows, wide), to_tiles[...])
         result = []
-        for c in range(tiles):
+        for c in each:
             span = slice(c // 2 * LANE, (c // 2 + 1) * LANE)
-            a, b = halves[0][:, span], halves[1][:, span]
+            a, b = both[:half_rows, span], both[half_rows:, span]
             if c % 2:
                 a = pltpu.roll(a, HALF, 1)
             else:
                 b = pltpu.roll(b, HALF, 1)
-            result.append(jnp.where(low_lanes, a, b).reshape(depth, SUB, LANE))
+            result.append(jnp.where(low_lanes, a, b))
         return result
 
     def place(p, carry):
-        for c, value in enumerate(tiled(p)):
-            first[p, 2 : depth + 2, c] = value
+        values = tiled(p)
+        for j in range(depth):
+            publish(first, p, j, [x[j * SUB : (j + 1) * SUB] for x in values])
         return carry
 
     lax.fori_loop(0, STATE, place, 0)
 
     def place_fixed(p, carry):
         for c, value in enumerate(tiled(STATE + p)):
-            mix[p, :, c] = value
+            mix[p, :, c] = value.reshape(depth, SUB, LANE)
         return carry
 
     lax.fori_loop(0, LEVELS + 1, place_fixed, 0)
-
-    def ghosts(buf):
-        def one(p, carry):
-            for c in range(tiles):
-                for to, source, ahead in ((0, depth, 0), (1, depth + 1, 0), (depth + 2, 2, 1), (depth + 3, 3, 1)):
-                    x = pltpu.roll(buf[p, source, c], HALF, 1)
-                    if ahead:
-                        buf[p, to, c] = jnp.where(lower_half, x, pltpu.roll(x, SUB - 1, 0))
-                    else:
-                        buf[p, to, c] = jnp.where(lower_half, pltpu.roll(x, 1, 0), x)
-            return carry
-
-        lax.fori_loop(0, STATE, one, 0)
-
-    def back(x):
-        return pltpu.roll(x, 1, 1)
-
-    def ahead(x):
-        return pltpu.roll(x, LANE - 1, 1)
+    mix[LEVELS] = TIMESTEP * mix[LEVELS]
 
     def face(before, a, b, after):
         return 7.0 * (a + b) - (before + after)
 
-    def prepare(q):
-        def weights(j, carry):
-            for c in range(tiles):
+    def weigh(q):
+        for j in range(-1, depth + 1):
+            beside = 1 if 0 <= j < depth else 0
+            for c in range(-beside, tiles + beside):
                 running = None
                 for k in range(LEVELS):
                     density = (
-                        (-THERMAL * 0.5 * GRAVITY) * q[k, j + 1, c]
-                        + (HALINE * 0.5 * GRAVITY) * q[LEVELS + k, j + 1, c]
+                        (-THERMAL * 0.5 * GRAVITY) * q[k, j + 2, c + edge]
+                        + (HALINE * 0.5 * GRAVITY) * q[LEVELS + k, j + 2, c + edge]
                     )
                     running = density if running is None else running + density
-                    press[k, j, c] = running
+                    press[k, j + 1, c + 1] = running
+
+    def advance(q, new):
+        weigh(q)
+
+        def level(k, carry):
+            zonal, merid = 2 * LEVELS + k, 3 * LEVELS + k
+            above, under = jnp.maximum(k - 1, 0), jnp.minimum(k + 1, LEVELS - 1)
+            for j in range(depth + 1):
+                for c in each:
+                    fast[j, c] = (q[merid, j + 1, c + edge] + q[merid, j + 2, c + edge]) * (1.0 / 24.0)
+            for j in range(depth):
+                for c in range(tiles + 1):
+                    along[j, c] = (q[zonal, j + 2, c + 1] + q[zonal, j + 2, c + 2]) * (1.0 / 24.0)
+            for f in range(FIELDS):
+                p = f * LEVELS + k
+
+                def line(j, p=p):
+                    return [q[p, j + 2, c + edge] for c in each]
+
+                lines = {j: line(j) for j in (-2, -1, 0)}
+                lower = None
+                for j in range(-1, depth):
+                    lines[j + 2] = line(j + 2)
+                    prev, here, succ, succ2 = (lines[j + d] for d in (-1, 0, 1, 2))
+                    upper = [fast[j + 1, c] * face(prev[c], here[c], succ[c], succ2[c]) for c in each]
+                    if j < 0:
+                        lower = upper
+                        continue
+                    ring = (
+                        [q[p, j + 2, 0], q[p, j + 2, 1]]
+                        + here
+                        + [q[p, j + 2, tiles + edge], q[p, j + 2, tiles + edge + 1]]
+                    )
+                    flux = [
+                        along[j, c] * face(ring[c], ring[c + 1], ring[c + 2], ring[c + 3])
+                        for c in range(tiles + 1)
+                    ]
+                    row = []
+                    for c in each:
+                        center = here[c]
+                        advection = (flux[c + 1] - flux[c]) + (upper[c] - lower[c])
+                        around = (ring[c + 1] + ring[c + 3]) + (prev[c] + succ[c])
+                        if f < 2:
+                            others = q[f * LEVELS + above, j + 2, c + edge] + q[f * LEVELS + under, j + 2, c + edge]
+                            mixed = around + (0.5 * others - 5.0 * center)
+                        else:
+                            mixed = around - 4.0 * center
+                        tendency = mix[k, j, c] * mixed - advection
+                        if f == 2:
+                            slope = press[k, j + 1, c + 2] - press[k, j + 1, c]
+                            tendency = tendency + (spin[j] * q[merid, j + 2, c + edge] - slope)
+                        elif f == 3:
+                            slope = press[k, j + 2, c + 1] - press[k, j, c + 1]
+                            tendency = tendency - (spin[j] * q[zonal, j + 2, c + edge] + slope)
+                        row.append(center + mix[LEVELS, j, c] * tendency)
+                    publish(new, p, j, row)
+                    lower = upper
             return carry
 
-        lax.fori_loop(0, depth + 2, weights, 0)
-
-        def speeds(j, carry):
-            for k in range(LEVELS):
-                for c in range(tiles):
-                    v = 3 * LEVELS + k
-                    fast[k, j, c] = (q[v, j + 1, c] + q[v, j + 2, c]) * (1.0 / 24.0)
-                u = [q[2 * LEVELS + k, j + 1, c] for c in range(tiles)]
-                u.append(ahead(u[0]))
-                for c in range(tiles):
-                    along[k, j, c] = (u[c] + u[c + 1]) * (1.0 / 24.0)
-            return carry
-
-        lax.fori_loop(0, depth + 1, speeds, 0)
-
-    chunk = depth // 2
-    each = range(tiles)
-
-    def advance(q, new):
-        def rows_of(i, carry):
-            base = i * chunk
-            for k in range(LEVELS):
-                for f in range(FIELDS):
-                    p = f * LEVELS + k
-
-                    def line(j, p=p):
-                        return [q[p, base + j + 2, c] for c in each]
-
-                    lines = {j: line(j) for j in (-2, -1, 0)}
-                    lower = None
-                    for j in range(-1, chunk):
-                        lines[j + 2] = line(j + 2)
-                        prev, here, succ, succ2 = (lines[j + d] for d in (-1, 0, 1, 2))
-                        upper = [
-                            fast[k, base + j + 1, c] * face(prev[c], here[c], succ[c], succ2[c]) for c in each
-                        ]
-                        if j < 0:
-                            lower = upper
-                            continue
-                        ring = [back(here[-1])] + here + [ahead(here[0]), ahead(here[1])]
-                        flux = [
-                            along[k, base + j + 1, c] * face(ring[c], ring[c + 1], ring[c + 2], ring[c + 3])
-                            for c in each
-                        ]
-                        flux = [back(flux[-1])] + flux
-                        if f == 2:
-                            load = [press[k, base + j + 1, c] for c in each]
-                            load = [back(load[-1])] + load + [ahead(load[0])]
-                        for c in each:
-                            center = here[c]
-                            advection = (flux[c + 1] - flux[c]) + (upper[c] - lower[c])
-                            around = (ring[c] + ring[c + 2]) + (prev[c] + succ[c])
-                            if f < 2:
-                                if k == 0 or k == LEVELS - 1:
-                                    other = q[p + (1 if k == 0 else -1), base + j + 2, c]
-                                    mixed = around + (0.5 * other - 4.5 * center)
-                                else:
-                                    others = q[p - 1, base + j + 2, c] + q[p + 1, base + j + 2, c]
-                                    mixed = around + (0.5 * others - 5.0 * center)
-                            else:
-                                mixed = around - 4.0 * center
-                            tendency = mix[k, base + j, c] * mixed - advection
-                            if f == 2:
-                                turned = spin[base + j] * q[p + LEVELS, base + j + 2, c]
-                                tendency = tendency + (turned - (load[c + 2] - load[c]))
-                            elif f == 3:
-                                turned = spin[base + j] * q[p - LEVELS, base + j + 2, c]
-                                slope = press[k, base + j + 2, c] - press[k, base + j, c]
-                                tendency = tendency - (turned + slope)
-                            wet = TIMESTEP * mix[LEVELS, base + j, c]
-                            new[p, base + j + 2, c] = center + wet * tendency
-                        lower = upper
-            return carry
-
-        lax.fori_loop(0, depth // chunk, rows_of, 0)
+        lax.fori_loop(0, LEVELS, level, 0)
 
     def pair(i, carry):
-        for q, new in ((first, second), (second, first)):
-            ghosts(q)
-            prepare(q)
-            advance(q, new)
+        advance(first, second)
+        advance(second, first)
         return carry
 
     lax.fori_loop(0, STEPS // 2, pair, 0)
 
     def gather(p, carry):
-        value = [first[p, 2 : depth + 2, c].reshape(half_rows, LANE) for c in each]
+        value = [first[p, 2 : depth + 2, c + edge].reshape(half_rows, LANE) for c in each]
+        halves = []
         for h in range(SIDE):
             parts = []
             for c in range(0, tiles, 2):
@@ -558,11 +545,14 @@
                 else:
                     b = jnp.zeros_like(a)
                 parts.append(jnp.where(low_lanes, a, b))
-            flat = exact_dot(jnp.concatenate(parts, axis=1), from_tiles[...])
+            halves.append(jnp.concatenate(parts, axis=1))
+        flat = exact_dot(jnp.concatenate(halves, axis=0), from_tiles[...])
+        for h in range(SIDE):
             for i in range(depth):
+                at = (h * depth + i) * SUB
                 for t in range(cols // LANE):
                     natural[t, p // LEVELS, p % LEVELS, pl.ds(h * depth + i, SUB, stride=SIDE * depth), :] = flat[
-                        i * SUB : (i + 1) * SUB, t * LANE : (t + 1) * LANE
+                        at : at + SUB, t * LANE : (t + 1) * LANE
                     ]
         return carry
 
@@ -622,13 +612,13 @@
             pltpu.VMEM((cols // LANE, FIELDS, LEVELS, ext, LANE), f32),
             pltpu.VMEM((cols // LANE, LEVELS + 1, ext, LANE), f32),
             pltpu.VMEM((PLANES, SIDE, depth, SUB, wide), f32),
-            pltpu.VMEM((STATE, depth + 4, tiles, SUB, LANE), f32),
-            pltpu.VMEM((STATE, depth + 4, tiles, SUB, LANE), f32),
+            pltpu.VMEM((STATE, depth + 4, tiles + 4, SUB, LANE), f32),
+            pltpu.VMEM((STATE, depth + 4, tiles + 4, SUB, LANE), f32),
             pltpu.VMEM((LEVELS + 1, depth, tiles, SUB, LANE), f32),
             pltpu.VMEM((depth, SUB, LANE), f32),
-            pltpu.VMEM((LEVELS, depth + 1, tiles, SUB, LANE), f32),
-            pltpu.VMEM((LEVELS, depth + 1, tiles, SUB, LANE), f32),
-            pltpu.VMEM((LEVELS, depth + 2, tiles, SUB, LANE), f32),
+            pltpu.VMEM((depth + 1, tiles, SUB, LANE), f32),
+            pltpu.VMEM((depth, tiles + 1, SUB, LANE), f32),
+            pltpu.VMEM((LEVELS, depth + 2, tiles + 2, SUB, LANE), f32),
             pltpu.VMEM((wide, wide), jnp.bfloat16),
             pltpu.VMEM((wide, cols), jnp.bfloat16),
             pltpu.SemaphoreType.DMA((2 * (cols // LANE),)),

time: 93.1 us -> 56.2 us (0.60)
  Pallas kernels: 89.6 us -> 52.7 us
    pallas_call x1, Pallas kernels: 75 us -> 38.1 us  [body(): pl.pallas_call(functools.partial(substeps_kernel, lons, lats), out_shape=...]
where the time goes in v2:
time: 56.2 us; the launch traced here: 56 us
  Pallas kernels  52.7 us (94%)
  local copies, waits for them, and re-layouts  3.32 us (6%)
    pallas_call x1, Pallas kernels, body(): pl.pallas_call(functools.partial(substeps_kernel, lons, lats), out_shape=...  38.1 us
    pallas_call x1, Pallas kernels, body(): pl.pallas_call(functools.partial(exchange_kernel, lons, lats), out_shape=...  14.6 us
    unnamed x12, local copies, waits for them, and re-layouts  3.32 us

profile of v2, /device:TPU:7, one launch (start us, length us, event | category | flops | bytes accessed | tf_op | source)
XLA Modules:
  0.0 56.0 jit_solution(15715823806016357067)
XLA Ops:
  0.0 0.0 copy-start
  0.0 1.4 %copy-done = f32[4,3,128,256]{3,2,1,0:T(8,128)S(1)} copy-done((f32[4,3,128,256]{3,2,1,0:T(8,128)S(1)}, f32[4,3,128,256]{3,2,1,0:T(8,128)}, u32[]{:S(2)}) %copy-start) | copy-done | bytes 1572888
  1.4 0.0 copy-start.2
  1.4 1.0 %copy-done.2 = f32[3,128,256]{2,1,0:T(8,128)S(1)} copy-done((f32[3,128,256]{2,1,0:T(8,128)S(1)}, f32[3,128,256]{2,1,0:T(8,128)}, u32[]{:S(2)}) %copy-start.2) | copy-done | bytes 393240
  2.4 0.0 copy-start.4
  2.4 0.9 %copy-done.4 = s32[128,256]{1,0:T(8,128)S(1)} copy-done((s32[128,256]{1,0:T(8,128)S(1)}, s32[128,256]{1,0:T(8,128)}, u32[]{:S(2)}) %copy-start.4) | copy-done | bytes 131096
  3.3 0.0 copy-start.1
  3.3 0.0 copy-start.3
  3.3 0.0 copy-start.5
  3.3 14.6 %exchange.1 = (f32[16,16,256]{2,1,0:T(8,128)S(1)}, f32[16,16,256]{2,1,0:T(8,128)S(1)}, f32[2,160,128]{2,1,0:T(8,128)S(1)}, f32[2,160,128]{2,1,0:T(8,128)S(1)}) custom-call(f32[4,3,128,256]{3,2,1,0:T(8,128)S(1)} %copy-done, f32[3,128,256]{2,1,0:T(8,128)S(1)} %copy-done.2, s32[128,256]{1,0:T(8,128)S(1)} %copy-done.4), custom_call_target="tpu_custom_call" | custom-call | tf_op jit(solution)/shard_map/exchange/pallas_call | solution.py:580
  17.9 0.0 copy-done.1
  17.9 0.0 copy-done.3
  17.9 0.0 copy-done.5
  17.9 38.1 %substeps.1 = f32[4,3,128,256]{3,2,1,0:T(8,128)} custom-call(f32[4,3,128,256]{3,2,1,0:T(8,128)S(1)} %copy-done.1, f32[3,128,256]{2,1,0:T(8,128)S(1)} %copy-done.3, s32[128,256]{1,0:T(8,128)S(1)} %copy-done.5, f32[16,16,256]{2,1,0:T(8,128)S(1)} %get-tuple-element.9.north, f32[16,16,256]{2,1,0:T(8,128)S(1)} %get-tuple-element.10.south, ...), custom_call_target="tpu_custom_call" | custom-call | tf_op jit(solution)/shard_map/substeps/pallas_call | solution.py:606
Async XLA Ops:
  0.0 1.4 %copy-start = (f32[4,3,128,256]{3,2,1,0:T(8,128)S(1)}, f32[4,3,128,256]{3,2,1,0:T(8,128)}, u32[]{:S(2)}) copy-start(f32[4,3,128,256]{3,2,1,0:T(8,128)} %state.3) | copy-start | bytes 4718596
  1.4 1.0 %copy-start.2 = (f32[3,128,256]{2,1,0:T(8,128)S(1)}, f32[3,128,256]{2,1,0:T(8,128)}, u32[]{:S(2)}) copy-start(f32[3,128,256]{2,1,0:T(8,128)} %mixing.3) | copy-start | bytes 1179652
  2.4 0.9 %copy-start.4 = (s32[128,256]{1,0:T(8,128)S(1)}, s32[128,256]{1,0:T(8,128)}, u32[]{:S(2)}) copy-start(s32[128,256]{1,0:T(8,128)} %land.3) | copy-start | bytes 393220
  3.3 14.6 %copy-start.1 = (f32[4,3,128,256]{3,2,1,0:T(8,128)S(1)}, f32[4,3,128,256]{3,2,1,0:T(8,128)}, u32[]{:S(2)}) copy-start(f32[4,3,128,256]{3,2,1,0:T(8,128)} %state.3) | copy-start | bytes 4718596
  3.3 14.6 %copy-start.3 = (f32[3,128,256]{2,1,0:T(8,128)S(1)}, f32[3,128,256]{2,1,0:T(8,128)}, u32[]{:S(2)}) copy-start(f32[3,128,256]{2,1,0:T(8,128)} %mixing.3) | copy-start | bytes 1179652
  3.3 14.6 %copy-start.5 = (s32[128,256]{1,0:T(8,128)S(1)}, s32[128,256]{1,0:T(8,128)}, u32[]{:S(2)}) copy-start(s32[128,256]{1,0:T(8,128)} %land.3) | copy-start | bytes 393220

commit v3 on v2

--- a/solution.py
+++ b/solution.py
@@ -41,8 +41,7 @@
     def reversal(size, group):
         i = lax.broadcasted_iota(jnp.int32, (size, size), 0)
         j = lax.broadcasted_iota(jnp.int32, (size, size), 1)
-        partner = (i // group) * group + (group - 1 - i % group)
-        return jnp.where(j == partner, 1.0, 0.0).astype(jnp.bfloat16)
+        return jnp.where(j == (i ^ (group - 1)), 1.0, 0.0).astype(jnp.bfloat16)
 
     def dot(a, b):
         return jnp.dot(a, b, preferred_element_type=jnp.float32)
@@ -56,8 +55,8 @@
 
 
 def exchange_kernel(
-    lons, lats, state, mixing, land, north, south, west, east,
-    to_west, to_east, to_north, to_south, corner_west, corner_east, send_sem, recv_sem, keep_sem,
+    lons, lats, state, mixing, land, natural, west, east, to_tiles, from_tiles, spin,
+    to_west, to_east, to_north, corner_west, corner_east, land_here, send_sem, recv_sem, keep_sem, load_sem,
 ):
     rows, cols = land.shape
     ext = rows + 2 * HALO
@@ -71,6 +70,30 @@
     across_east = lax.rem(2 * lons - 2 - lon, lons)
     across_west = lax.rem(lons - lon, lons)
 
+    low = pl.ds(0, HALO)
+    high = pl.ds(ext - HALO, HALO)
+    middle = pl.ds(HALO, rows)
+    lane_tiles = cols // LANE
+
+    loads = [pltpu.make_async_copy(land, land_here, load_sem.at[0])]
+    for t in range(lane_tiles):
+        span = pl.ds(t * LANE, LANE)
+        for f in range(FIELDS):
+            loads.append(
+                pltpu.make_async_copy(
+                    state.at[f, :, :, span],
+                    natural.at[t, pl.ds(f * LEVELS, LEVELS), middle, :],
+                    load_sem.at[len(loads)],
+                )
+            )
+        loads.append(
+            pltpu.make_async_copy(
+                mixing.at[:, :, span], natural.at[t, pl.ds(STATE, LEVELS), middle, :], load_sem.at[len(loads)]
+            )
+        )
+    for c in loads:
+        c.start()
+
     barrier = pltpu.get_barrier_semaphore()
 
     def greet(x, y):
@@ -101,17 +124,10 @@
         def _():
             greet(across_west, lat)
 
-    def plane(p, row_slice, col_slice):
-        if p < STATE:
-            return state[p // LEVELS, p % LEVELS, row_slice, col_slice]
-        if p < STATE + LEVELS:
-            return mixing[p - STATE, row_slice, col_slice]
-        return land[row_slice, col_slice].astype(jnp.float32)
-
-    everything = slice(0, cols)
-    for p in range(PLANES):
-        to_south[p] = plane(p, slice(0, HALO), everything)
-        to_north[p] = plane(p, slice(rows - HALO, rows), everything)
+    for c in loads:
+        c.wait()
+    for t in range(lane_tiles):
+        natural[t, PLANES - 1, HALO : HALO + rows, :] = land_here[:, t * LANE : (t + 1) * LANE].astype(jnp.float32)
 
     lane = lax.broadcasted_iota(jnp.int32, (rows, LANE), 1)
     for g in range(GROUPS):
@@ -120,8 +136,8 @@
         for slot in range(PER_TILE):
             p = g * PER_TILE + slot
             here = (lane >= slot * HALO) & (lane < (slot + 1) * HALO)
-            first = plane(p, slice(0, rows), slice(0, LANE))
-            last = plane(p, slice(0, rows), slice(cols - LANE, cols))
+            first = natural[0, p, HALO : HALO + rows, :]
+            last = natural[lane_tiles - 1, p, HALO : HALO + rows, :]
             if slot:
                 first = pltpu.roll(first, slot * HALO, 1)
             if (slot + 1) * HALO != LANE:
@@ -133,11 +149,14 @@
 
     @pl.when(northmost)
     def _():
-        full = to_north[...].reshape(PLANES * HALO, cols)
-        index = lax.broadcasted_iota(jnp.int32, full.shape, 0) // HALO
+        top = [natural[t, :, rows : rows + HALO, :].reshape(PLANES * HALO, LANE) for t in range(lane_tiles)]
+        full = jnp.concatenate(top, axis=1)
+        index = lax.broadcasted_iota(jnp.int32, full.shape, 0) >> (HALO.bit_length() - 1)
         odd = (index >= 2 * LEVELS) & (index < STATE)
         full = flipped((full, cols))
-        to_north[...] = jnp.where(odd, -full, full).reshape(PLANES, HALO, cols)
+        full = jnp.where(odd, -full, full)
+        for t in range(lane_tiles):
+            to_north[t] = full[:, t * LANE : (t + 1) * LANE].reshape(PLANES, HALO, LANE)
         shape = (GROUPS * HALO, LANE)
         index = (
             lax.broadcasted_iota(jnp.int32, shape, 0) // HALO * PER_TILE
@@ -170,10 +189,6 @@
         )
         pl.semaphore_wait(barrier, 2 + 3 * has_south.astype(jnp.int32) + folds)
 
-    low = pl.ds(0, HALO)
-    high = pl.ds(ext - HALO, HALO)
-    middle = pl.ds(HALO, rows)
-
     def copy(src, dst, send, recv, x, y):
         return pltpu.make_async_remote_copy(
             src_ref=src,
@@ -192,20 +207,20 @@
 
     def southward():
         return (
-            copy(to_south, north, 2, 2, lon, lat - 1),
+            copy(natural.at[:, :, pl.ds(HALO, HALO), :], natural.at[:, :, high, :], 2, 2, lon, lat - 1),
             copy(to_west.at[:, low, :], east.at[:, high, :], 3, 3, left, lat - 1),
             copy(to_east.at[:, low, :], west.at[:, high, :], 4, 4, right, lat - 1),
         )
 
     def northward():
         return (
-            copy(to_north, south, 5, 5, lon, lat + 1),
+            copy(natural.at[:, :, pl.ds(rows, HALO), :], natural.at[:, :, low, :], 5, 5, lon, lat + 1),
             copy(corner_west, east.at[:, low, :], 6, 6, left, lat + 1),
             copy(corner_east, west.at[:, low, :], 7, 7, right, lat + 1),
         )
 
     def folded():
-        return copy(to_north, north, 5, 2, across, lat)
+        return copy(to_north, natural.at[:, :, high, :], 5, 2, across, lat)
 
     def folded_east():
         return copy(corner_east, east.at[:, high, :], 6, 3, across_east, lat)
@@ -254,9 +269,29 @@
 
     @pl.when(jnp.logical_not(has_south))
     def _():
-        south[...] = jnp.zeros(south.shape, jnp.float32)
+        natural[:, :, 0:HALO, :] = jnp.zeros((lane_tiles, PLANES, HALO, LANE), jnp.float32)
         west[:, 0:HALO, :] = jnp.zeros((GROUPS, HALO, LANE), jnp.float32)
         east[:, 0:HALO, :] = jnp.zeros((GROUPS, HALO, LANE), jnp.float32)
+
+    tiles = -(-(cols + 2 * HALO) // HALF)
+    depth = spin.shape[0]
+    def selection(shape, tile_dim):
+        j = lax.broadcasted_iota(jnp.int32, shape, tile_dim)
+        n = lax.broadcasted_iota(jnp.int32, shape, 1 - tile_dim)
+        home = tiles * (j & (HALF - 1)) + (j >> (HALF.bit_length() - 1)) - HALO
+        home = jnp.where(home < 0, home + tiles * HALF, home)
+        return jnp.where((n == home) & (j < tiles * HALF), 1.0, 0.0).astype(jnp.bfloat16)
+
+    to_tiles[...] = selection(to_tiles.shape, 1)
+    from_tiles[...] = selection(from_tiles.shape, 0)
+
+    r = lax.broadcasted_iota(jnp.int32, (depth, SUB, LANE), 0)
+    s = lax.broadcasted_iota(jnp.int32, (depth, SUB, LANE), 1)
+    h = lax.broadcasted_iota(jnp.int32, (depth, SUB, LANE), 2) >> (HALF.bit_length() - 1)
+    total = rows * lats
+    row = lat * rows - HALO + (SIDE * s + h) * depth + r
+    row = jnp.where(row >= total, 2 * total - 1 - row, row).astype(jnp.float32)
+    spin[...] = jnp.sin(jnp.pi * (row + 0.5) / total - jnp.pi / 2)
 
     westward().wait()
     eastward().wait()
@@ -304,63 +339,14 @@
 
 
 def substeps_kernel(
-    lons, lats, state, mixing, land, north, south, west, east, out,
-    natural, fixed, joined, first, second, mix, spin, fast, along, press, to_tiles, from_tiles, sems, out_sem,
+    natural, west, east, to_tiles, from_tiles, spin, out,
+    joined, first, second, mix, fast, along, press, result, out_sem,
 ):
-    rows, cols = land.shape
-    ext = rows + 2 * HALO
+    lane_tiles, _, ext, _ = natural.shape
+    rows, cols = ext - 2 * HALO, lane_tiles * LANE
     depth = spin.shape[0]
     tiles = mix.shape[2]
-    lat = lax.axis_index("lat")
     middle = pl.ds(HALO, rows)
-
-    loads = [
-        c
-        for t in range(cols // LANE)
-        for c in (
-            pltpu.make_async_copy(
-                state.at[:, :, :, pl.ds(t * LANE, LANE)], natural.at[t, :, :, middle, :], sems.at[2 * t]
-            ),
-            pltpu.make_async_copy(
-                mixing.at[:, :, pl.ds(t * LANE, LANE)],
-                fixed.at[t, pl.ds(0, LEVELS), middle, :],
-                sems.at[2 * t + 1],
-            ),
-        )
-    ]
-    for c in loads:
-        c.start()
-
-    def selection(shape, tile_dim):
-        j = lax.broadcasted_iota(jnp.int32, shape, tile_dim)
-        n = lax.broadcasted_iota(jnp.int32, shape, 1 - tile_dim)
-        home = tiles * (j & (HALF - 1)) + j // HALF - HALO
-        home = jnp.where(home < 0, home + tiles * HALF, home)
-        return jnp.where((n == home) & (j < tiles * HALF), 1.0, 0.0).astype(jnp.bfloat16)
-
-    to_tiles[...] = selection(to_tiles.shape, 1)
-    from_tiles[...] = selection(from_tiles.shape, 0)
-
-    r = lax.broadcasted_iota(jnp.int32, (depth, SUB, LANE), 0)
-    s = lax.broadcasted_iota(jnp.int32, (depth, SUB, LANE), 1)
-    h = lax.broadcasted_iota(jnp.int32, (depth, SUB, LANE), 2) // HALF
-    total = rows * lats
-    row = lat * rows - HALO + (SIDE * s + h) * depth + r
-    row = jnp.where(row >= total, 2 * total - 1 - row, row).astype(jnp.float32)
-    spin[...] = jnp.sin(jnp.pi * (row + 0.5) / total - jnp.pi / 2)
-
-    for t in range(cols // LANE):
-        span = slice(t * LANE, (t + 1) * LANE)
-        for f in range(FIELDS):
-            for k in range(LEVELS):
-                natural[t, f, k, 0:HALO, :] = south[f * LEVELS + k, :, span]
-                natural[t, f, k, ext - HALO : ext, :] = north[f * LEVELS + k, :, span]
-        for p in range(LEVELS + 1):
-            fixed[t, p, 0:HALO, :] = south[STATE + p, :, span]
-            fixed[t, p, ext - HALO : ext, :] = north[STATE + p, :, span]
-        fixed[t, LEVELS, HALO : HALO + rows, :] = land[:, span].astype(jnp.float32)
-    for c in loads:
-        c.wait()
 
     lane = lax.broadcasted_iota(jnp.int32, (SUB, LANE), 1)
     lower_half = lane < HALF
@@ -382,11 +368,7 @@
                         lane < HALO, e, jnp.where((lane >= west_at) & (lane < west_at + HALO), w, 0.0)
                     )
                     for t in range(cols // LANE):
-                        if p < STATE:
-                            value = natural[t, p // LEVELS, p % LEVELS, picked, :]
-                        else:
-                            value = fixed[t, p - STATE, picked, :]
-                        joined[p, h, i, :, t * LANE : (t + 1) * LANE] = value
+                        joined[p, h, i, :, t * LANE : (t + 1) * LANE] = natural[t, p, picked, :]
                     joined[p, h, i, :, cols : cols + LANE] = side
         return carry
 
@@ -434,20 +416,18 @@
             result.append(jnp.where(low_lanes, a, b))
         return result
 
-    def place(p, carry):
-        values = tiled(p)
-        for j in range(depth):
-            publish(first, p, j, [x[j * SUB : (j + 1) * SUB] for x in values])
+    def place(f, carry):
+        for k in range(LEVELS):
+            p = f * LEVELS + k
+            values = tiled(p)
+            for j in range(depth):
+                publish(first, p, j, [x[j * SUB : (j + 1) * SUB] for x in values])
         return carry
 
-    lax.fori_loop(0, STATE, place, 0)
-
-    def place_fixed(p, carry):
+    lax.fori_loop(0, FIELDS, place, 0)
+    for p in range(LEVELS + 1):
         for c, value in enumerate(tiled(STATE + p)):
             mix[p, :, c] = value.reshape(depth, SUB, LANE)
-        return carry
-
-    lax.fori_loop(0, LEVELS + 1, place_fixed, 0)
     mix[LEVELS] = TIMESTEP * mix[LEVELS]
 
     def face(before, a, b, after):
@@ -533,7 +513,12 @@
 
     lax.fori_loop(0, STEPS // 2, pair, 0)
 
-    def gather(p, carry):
+    def gather(f, carry):
+        for k in range(LEVELS):
+            collect(f, k, f * LEVELS + k)
+        return carry
+
+    def collect(f, k, p):
         value = [first[p, 2 : depth + 2, c + edge].reshape(half_rows, LANE) for c in each]
         halves = []
         for h in range(SIDE):
@@ -551,15 +536,14 @@
             for i in range(depth):
                 at = (h * depth + i) * SUB
                 for t in range(cols // LANE):
-                    natural[t, p // LEVELS, p % LEVELS, pl.ds(h * depth + i, SUB, stride=SIDE * depth), :] = flat[
+                    result[t, f, k, pl.ds(h * depth + i, SUB, stride=SIDE * depth), :] = flat[
                         at : at + SUB, t * LANE : (t + 1) * LANE
                     ]
-        return carry
-
-    lax.fori_loop(0, STATE, gather, 0)
+
+    lax.fori_loop(0, FIELDS, gather, 0)
     stores = [
         pltpu.make_async_copy(
-            natural.at[t, :, :, middle, :], out.at[:, :, :, pl.ds(t * LANE, LANE)], out_sem.at[t]
+            result.at[t, :, :, middle, :], out.at[:, :, :, pl.ds(t * LANE, LANE)], out_sem.at[t]
         )
         for t in range(cols // LANE)
     ]
@@ -576,57 +560,56 @@
     tiles = -(-(cols + 2 * HALO) // HALF)
     f32 = jnp.float32
     vmem = pl.BlockSpec(memory_space=pltpu.VMEM)
-    hbm = pl.BlockSpec(memory_space=pl.ANY)
-    halos = pl.pallas_call(
+    hbm = pl.BlockSpec(memory_space=pltpu.HBM)
+    lane_tiles = cols // LANE
+    extended = pl.pallas_call(
         functools.partial(exchange_kernel, lons, lats),
         out_shape=[
-            jax.ShapeDtypeStruct((PLANES, HALO, cols), f32),
-            jax.ShapeDtypeStruct((PLANES, HALO, cols), f32),
+            jax.ShapeDtypeStruct((lane_tiles, PLANES, ext, LANE), f32),
             jax.ShapeDtypeStruct((GROUPS, ext, LANE), f32),
             jax.ShapeDtypeStruct((GROUPS, ext, LANE), f32),
+            jax.ShapeDtypeStruct((wide, wide), jnp.bfloat16),
+            jax.ShapeDtypeStruct((wide, cols), jnp.bfloat16),
+            jax.ShapeDtypeStruct((depth, SUB, LANE), f32),
         ],
-        in_specs=[vmem] * 3,
-        out_specs=[vmem] * 4,
+        in_specs=[hbm] * 3,
+        out_specs=[vmem] * 6,
         scratch_shapes=[
             pltpu.VMEM((GROUPS, rows, LANE), f32),
             pltpu.VMEM((GROUPS, rows, LANE), f32),
-            pltpu.VMEM((PLANES, HALO, cols), f32),
-            pltpu.VMEM((PLANES, HALO, cols), f32),
+            pltpu.VMEM((lane_tiles, PLANES, HALO, LANE), f32),
             pltpu.VMEM((GROUPS, HALO, LANE), f32),
             pltpu.VMEM((GROUPS, HALO, LANE), f32),
+            pltpu.VMEM((rows, cols), jnp.int32),
             pltpu.SemaphoreType.DMA((8,)),
             pltpu.SemaphoreType.DMA((8,)),
             pltpu.SemaphoreType.DMA((2,)),
+            pltpu.SemaphoreType.DMA((1 + lane_tiles * (FIELDS + 1),)),
         ],
         compiler_params=pltpu.CompilerParams(
-            collective_id=0, has_side_effects=True, vmem_limit_bytes=32 * 2**20
+            collective_id=0, has_side_effects=True, vmem_limit_bytes=24 * 2**20
         ),
         name="exchange",
     )(ocean_state, mixing, land_sea)
     return pl.pallas_call(
-        functools.partial(substeps_kernel, lons, lats),
+        substeps_kernel,
         out_shape=jax.ShapeDtypeStruct(ocean_state.shape, f32),
-        in_specs=[hbm, hbm] + [vmem] * 5,
+        in_specs=[vmem] * 6,
         out_specs=hbm,
         scratch_shapes=[
-            pltpu.VMEM((cols // LANE, FIELDS, LEVELS, ext, LANE), f32),
-            pltpu.VMEM((cols // LANE, LEVELS + 1, ext, LANE), f32),
             pltpu.VMEM((PLANES, SIDE, depth, SUB, wide), f32),
             pltpu.VMEM((STATE, depth + 4, tiles + 4, SUB, LANE), f32),
             pltpu.VMEM((STATE, depth + 4, tiles + 4, SUB, LANE), f32),
             pltpu.VMEM((LEVELS + 1, depth, tiles, SUB, LANE), f32),
-            pltpu.VMEM((depth, SUB, LANE), f32),
             pltpu.VMEM((depth + 1, tiles, SUB, LANE), f32),
             pltpu.VMEM((depth, tiles + 1, SUB, LANE), f32),
             pltpu.VMEM((LEVELS, depth + 2, tiles + 2, SUB, LANE), f32),
-            pltpu.VMEM((wide, wide), jnp.bfloat16),
-            pltpu.VMEM((wide, cols), jnp.bfloat16),
-            pltpu.SemaphoreType.DMA((2 * (cols // LANE),)),
-            pltpu.SemaphoreType.DMA((cols // LANE,)),
+            pltpu.VMEM((lane_tiles, FIELDS, LEVELS, ext, LANE), f32),
+            pltpu.SemaphoreType.DMA((lane_tiles,)),
         ],
-        compiler_params=pltpu.CompilerParams(vmem_limit_bytes=48 * 2**20),
+        compiler_params=pltpu.CompilerParams(vmem_limit_bytes=32 * 2**20),
         name="substeps",
-    )(ocean_state, mixing, land_sea, *halos)
+    )(*extended)
 
 
 def solution(mesh):

time: 56.2 us -> 51.1 us (0.909)
  Pallas kernels: 52.7 us -> 47.6 us
    pallas_call x1, Pallas kernels: 38.1 us -> 32.6 us  [body(): pl.pallas_call(substeps_kernel, out_shape=jax.ShapeDtypeStruct(ocean_stat...]
    unnamed x12 -> x6, local copies, waits for them, and re-layouts: 3.32 us -> 3.31 us
where the time goes in v3:
time: 51.1 us; the launch traced here: 50.9 us
  Pallas kernels  47.6 us (93%)
  local copies, waits for them, and re-layouts  3.31 us (6%)
    pallas_call x1, Pallas kernels, body(): pl.pallas_call(substeps_kernel, out_shape=jax.ShapeDtypeStruct(ocean_stat...  32.6 us
    pallas_call x1, Pallas kernels, body(): pl.pallas_call(functools.partial(exchange_kernel, lons, lats), out_shape=...  15 us
    unnamed x6, local copies, waits for them, and re-layouts  3.31 us

profile of v3, /device:TPU:7, one launch (start us, length us, event | category | flops | bytes accessed | tf_op | source)
XLA Modules:
  0.0 50.9 jit_solution(10835203571838242232)
XLA Ops:
  0.0 0.0 copy-start
  0.0 1.4 %copy-done = f32[4,3,128,256]{3,2,1,0:T(8,128)S(1)} copy-done((f32[4,3,128,256]{3,2,1,0:T(8,128)S(1)}, f32[4,3,128,256]{3,2,1,0:T(8,128)}, u32[]{:S(2)}) %copy-start) | copy-done | bytes 1572888
  1.4 0.0 copy-start.1
  1.4 1.0 %copy-done.1 = f32[3,128,256]{2,1,0:T(8,128)S(1)} copy-done((f32[3,128,256]{2,1,0:T(8,128)S(1)}, f32[3,128,256]{2,1,0:T(8,128)}, u32[]{:S(2)}) %copy-start.1) | copy-done | bytes 393240
  2.4 0.0 copy-start.2
  2.4 0.9 %copy-done.2 = s32[128,256]{1,0:T(8,128)S(1)} copy-done((s32[128,256]{1,0:T(8,128)S(1)}, s32[128,256]{1,0:T(8,128)}, u32[]{:S(2)}) %copy-start.2) | copy-done | bytes 131096
  3.3 15.0 %exchange.1 = (f32[2,16,160,128]{3,2,1,0:T(8,128)S(1)}, f32[2,160,128]{2,1,0:T(8,128)S(1)}, f32[2,160,128]{2,1,0:T(8,128)S(1)}, bf16[384,384]{1,0:T(8,128)(2,1)S...) custom-call(f32[4,3,128,256]{3,2,1,0:T(8,128)S(1)} %copy-done, f32[3,128,256]{2,1,0:T(8,128)S(1)} %copy-done.1, ...), custom_call_target="tpu_custom_call" | custom-call | tf_op jit(solution)/shard_map/exchange/pallas_call | solution.py:565
  18.3 32.6 %substeps.1 = f32[4,3,128,256]{3,2,1,0:T(8,128)} custom-call(f32[2,16,160,128]{3,2,1,0:T(8,128)S(1)} %get-tuple-element.11.natural, f32[2,160,128]{2,1,0:T(8,128)S(1)} %get-tuple-element.12.west, f32[2,160,128]{2,1,0:T(8,128)S(1)} %get-tuple-element.13.east, bf16[384,384]{1,0:T(8,128)(2,1)S(1)} %get-tuple-element.14.to_tiles, ...), custom_call_target="tpu_custom_call" | custom-call | tf_op jit(solution)/shard_map/substeps/pallas_call | solution.py:594
Async XLA Ops:
  0.0 1.4 %copy-start = (f32[4,3,128,256]{3,2,1,0:T(8,128)S(1)}, f32[4,3,128,256]{3,2,1,0:T(8,128)}, u32[]{:S(2)}) copy-start(f32[4,3,128,256]{3,2,1,0:T(8,128)} %state.1) | copy-start | bytes 4718596
  1.4 1.0 %copy-start.1 = (f32[3,128,256]{2,1,0:T(8,128)S(1)}, f32[3,128,256]{2,1,0:T(8,128)}, u32[]{:S(2)}) copy-start(f32[3,128,256]{2,1,0:T(8,128)} %mixing.1) | copy-start | bytes 1179652
  2.4 0.9 %copy-start.2 = (s32[128,256]{1,0:T(8,128)S(1)}, s32[128,256]{1,0:T(8,128)}, u32[]{:S(2)}) copy-start(s32[128,256]{1,0:T(8,128)} %land.1) | copy-start | bytes 393220

commit v4 on v3

--- a/solution.py
+++ b/solution.py
@@ -129,6 +129,90 @@
     for t in range(lane_tiles):
         natural[t, PLANES - 1, HALO : HALO + rows, :] = land_here[:, t * LANE : (t + 1) * LANE].astype(jnp.float32)
 
+    @pl.when(northmost)
+    def _():
+        top = [natural[t, :, rows : rows + HALO, :].reshape(PLANES * HALO, LANE) for t in range(lane_tiles)]
+        full = jnp.concatenate(top, axis=1)
+        index = lax.broadcasted_iota(jnp.int32, full.shape, 0) >> (HALO.bit_length() - 1)
+        odd = (index >= 2 * LEVELS) & (index < STATE)
+        full = flipped((full, cols))
+        full = jnp.where(odd, -full, full)
+        for t in range(lane_tiles):
+            to_north[t] = full[:, t * LANE : (t + 1) * LANE].reshape(PLANES, HALO, LANE)
+    @pl.when(has_south & jnp.logical_not(northmost))
+    def _():
+        pl.semaphore_wait(barrier, 8)
+
+    @pl.when(jnp.logical_not(has_south) & jnp.logical_not(northmost))
+    def _():
+        pl.semaphore_wait(barrier, 5)
+
+    @pl.when(northmost)
+    def _():
+        folds = (
+            1
+            + (across_east != lon).astype(jnp.int32)
+            + (across_west != lon).astype(jnp.int32)
+        )
+        pl.semaphore_wait(barrier, 2 + 3 * has_south.astype(jnp.int32) + folds)
+
+    def copy(src, dst, send, recv, x, y):
+        return pltpu.make_async_remote_copy(
+            src_ref=src,
+            dst_ref=dst,
+            send_sem=send_sem.at[send],
+            recv_sem=recv_sem.at[recv],
+            device_id=(x, y),
+            device_id_type=pl.DeviceIdType.MESH,
+        )
+
+    def westward():
+        return copy(to_west, east.at[:, middle, :], 0, 1, left, lat)
+
+    def eastward():
+        return copy(to_east, west.at[:, middle, :], 1, 0, right, lat)
+
+    def southward():
+        return (
+            copy(natural.at[:, :, pl.ds(HALO, HALO), :], natural.at[:, :, high, :], 2, 2, lon, lat - 1),
+            copy(to_west.at[:, low, :], east.at[:, high, :], 3, 3, left, lat - 1),
+            copy(to_east.at[:, low, :], west.at[:, high, :], 4, 4, right, lat - 1),
+        )
+
+    def northward():
+        return (
+            copy(natural.at[:, :, pl.ds(rows, HALO), :], natural.at[:, :, low, :], 5, 5, lon, lat + 1),
+            copy(corner_west, east.at[:, low, :], 6, 6, left, lat + 1),
+            copy(corner_east, west.at[:, low, :], 7, 7, right, lat + 1),
+        )
+
+    def folded():
+        return copy(to_north, natural.at[:, :, high, :], 5, 2, across, lat)
+
+    def folded_east():
+        return copy(corner_east, east.at[:, high, :], 6, 3, across_east, lat)
+
+    def folded_west():
+        return copy(corner_west, west.at[:, high, :], 7, 4, across_west, lat)
+
+    def kept_east():
+        return pltpu.make_async_copy(corner_east, east.at[:, high, :], keep_sem.at[0])
+
+    def kept_west():
+        return pltpu.make_async_copy(corner_west, west.at[:, high, :], keep_sem.at[1])
+
+    @pl.when(northmost)
+    def _():
+        folded().start()
+
+    @pl.when(has_south)
+    def _():
+        southward()[0].start()
+
+    @pl.when(jnp.logical_not(northmost))
+    def _():
+        northward()[0].start()
+
     lane = lax.broadcasted_iota(jnp.int32, (rows, LANE), 1)
     for g in range(GROUPS):
         packed_west = jnp.zeros((rows, LANE), jnp.float32)
@@ -147,16 +231,11 @@
         to_west[g] = packed_west
         to_east[g] = packed_east
 
+    westward().start()
+    eastward().start()
+
     @pl.when(northmost)
     def _():
-        top = [natural[t, :, rows : rows + HALO, :].reshape(PLANES * HALO, LANE) for t in range(lane_tiles)]
-        full = jnp.concatenate(top, axis=1)
-        index = lax.broadcasted_iota(jnp.int32, full.shape, 0) >> (HALO.bit_length() - 1)
-        odd = (index >= 2 * LEVELS) & (index < STATE)
-        full = flipped((full, cols))
-        full = jnp.where(odd, -full, full)
-        for t in range(lane_tiles):
-            to_north[t] = full[:, t * LANE : (t + 1) * LANE].reshape(PLANES, HALO, LANE)
         shape = (GROUPS * HALO, LANE)
         index = (
             lax.broadcasted_iota(jnp.int32, shape, 0) // HALO * PER_TILE
@@ -172,82 +251,18 @@
         corner_west[...] = to_west[:, rows - HALO :, :]
         corner_east[...] = to_east[:, rows - HALO :, :]
 
-    @pl.when(has_south & jnp.logical_not(northmost))
-    def _():
-        pl.semaphore_wait(barrier, 8)
-
-    @pl.when(jnp.logical_not(has_south) & jnp.logical_not(northmost))
-    def _():
-        pl.semaphore_wait(barrier, 5)
+    @pl.when(has_south)
+    def _():
+        for c in southward()[1:]:
+            c.start()
+
+    @pl.when(jnp.logical_not(northmost))
+    def _():
+        for c in northward()[1:]:
+            c.start()
 
     @pl.when(northmost)
     def _():
-        folds = (
-            1
-            + (across_east != lon).astype(jnp.int32)
-            + (across_west != lon).astype(jnp.int32)
-        )
-        pl.semaphore_wait(barrier, 2 + 3 * has_south.astype(jnp.int32) + folds)
-
-    def copy(src, dst, send, recv, x, y):
-        return pltpu.make_async_remote_copy(
-            src_ref=src,
-            dst_ref=dst,
-            send_sem=send_sem.at[send],
-            recv_sem=recv_sem.at[recv],
-            device_id=(x, y),
-            device_id_type=pl.DeviceIdType.MESH,
-        )
-
-    def westward():
-        return copy(to_west, east.at[:, middle, :], 0, 1, left, lat)
-
-    def eastward():
-        return copy(to_east, west.at[:, middle, :], 1, 0, right, lat)
-
-    def southward():
-        return (
-            copy(natural.at[:, :, pl.ds(HALO, HALO), :], natural.at[:, :, high, :], 2, 2, lon, lat - 1),
-            copy(to_west.at[:, low, :], east.at[:, high, :], 3, 3, left, lat - 1),
-            copy(to_east.at[:, low, :], west.at[:, high, :], 4, 4, right, lat - 1),
-        )
-
-    def northward():
-        return (
-            copy(natural.at[:, :, pl.ds(rows, HALO), :], natural.at[:, :, low, :], 5, 5, lon, lat + 1),
-            copy(corner_west, east.at[:, low, :], 6, 6, left, lat + 1),
-            copy(corner_east, west.at[:, low, :], 7, 7, right, lat + 1),
-        )
-
-    def folded():
-        return copy(to_north, natural.at[:, :, high, :], 5, 2, across, lat)
-
-    def folded_east():
-        return copy(corner_east, east.at[:, high, :], 6, 3, across_east, lat)
-
-    def folded_west():
-        return copy(corner_west, west.at[:, high, :], 7, 4, across_west, lat)
-
-    def kept_east():
-        return pltpu.make_async_copy(corner_east, east.at[:, high, :], keep_sem.at[0])
-
-    def kept_west():
-        return pltpu.make_async_copy(corner_west, west.at[:, high, :], keep_sem.at[1])
-
-    @pl.when(has_south)
-    def _():
-        for c in southward():
-            c.start()
-
-    @pl.when(jnp.logical_not(northmost))
-    def _():
-        for c in northward():
-            c.start()
-
-    @pl.when(northmost)
-    def _():
-        folded().start()
-
         @pl.when(across_east != lon)
         def _():
             folded_east().start()
@@ -263,9 +278,6 @@
         @pl.when(across_west == lon)
         def _():
             kept_west().start()
-
-    westward().start()
-    eastward().start()
 
     @pl.when(jnp.logical_not(has_south))
     def _():
@@ -346,8 +358,6 @@
     rows, cols = ext - 2 * HALO, lane_tiles * LANE
     depth = spin.shape[0]
     tiles = mix.shape[2]
-    middle = pl.ds(HALO, rows)
-
     lane = lax.broadcasted_iota(jnp.int32, (SUB, LANE), 1)
     lower_half = lane < HALF
     west_at = tiles * HALF - cols - HALO
@@ -430,9 +440,6 @@
             mix[p, :, c] = value.reshape(depth, SUB, LANE)
     mix[LEVELS] = TIMESTEP * mix[LEVELS]
 
-    def face(before, a, b, after):
-        return 7.0 * (a + b) - (before + after)
-
     def weigh(q):
         for j in range(-1, depth + 1):
             beside = 1 if 0 <= j < depth else 0
@@ -454,10 +461,10 @@
             above, under = jnp.maximum(k - 1, 0), jnp.minimum(k + 1, LEVELS - 1)
             for j in range(depth + 1):
                 for c in each:
-                    fast[j, c] = (q[merid, j + 1, c + edge] + q[merid, j + 2, c + edge]) * (1.0 / 24.0)
+                    fast[j, c] = (q[merid, j + 1, c + edge] + q[merid, j + 2, c + edge]) * (1.0 / 3.0)
             for j in range(depth):
                 for c in range(tiles + 1):
-                    along[j, c] = (q[zonal, j + 2, c + 1] + q[zonal, j + 2, c + 2]) * (1.0 / 24.0)
+                    along[j, c] = (q[zonal, j + 2, c + 1] + q[zonal, j + 2, c + 2]) * (1.0 / 3.0)
             for f in range(FIELDS):
                 p = f * LEVELS + k
 
@@ -465,11 +472,15 @@
                     return [q[p, j + 2, c + edge] for c in each]
 
                 lines = {j: line(j) for j in (-2, -1, 0)}
+                near = {-1: [lines[-2][c] + lines[0][c] for c in each]}
+                bent = {-1: [lines[-1][c] - 0.125 * near[-1][c] for c in each]}
                 lower = None
                 for j in range(-1, depth):
                     lines[j + 2] = line(j + 2)
-                    prev, here, succ, succ2 = (lines[j + d] for d in (-1, 0, 1, 2))
-                    upper = [fast[j + 1, c] * face(prev[c], here[c], succ[c], succ2[c]) for c in each]
+                    here = lines[j]
+                    near[j + 1] = [lines[j][c] + lines[j + 2][c] for c in each]
+                    bent[j + 1] = [lines[j + 1][c] - 0.125 * near[j + 1][c] for c in each]
+                    upper = [fast[j + 1, c] * (bent[j][c] + bent[j + 1][c]) for c in each]
                     if j < 0:
                         lower = upper
                         continue
@@ -478,15 +489,14 @@
                         + here
                         + [q[p, j + 2, tiles + edge], q[p, j + 2, tiles + edge + 1]]
                     )
-                    flux = [
-                        along[j, c] * face(ring[c], ring[c + 1], ring[c + 2], ring[c + 3])
-                        for c in range(tiles + 1)
-                    ]
+                    beside = [ring[c] + ring[c + 2] for c in range(tiles + 2)]
+                    curved = [ring[c + 1] - 0.125 * beside[c] for c in range(tiles + 2)]
+                    flux = [along[j, c] * (curved[c] + curved[c + 1]) for c in range(tiles + 1)]
                     row = []
                     for c in each:
                         center = here[c]
                         advection = (flux[c + 1] - flux[c]) + (upper[c] - lower[c])
-                        around = (ring[c + 1] + ring[c + 3]) + (prev[c] + succ[c])
+                        around = beside[c + 1] + near[j][c]
                         if f < 2:
                             others = q[f * LEVELS + above, j + 2, c + edge] + q[f * LEVELS + under, j + 2, c + edge]
                             mixed = around + (0.5 * others - 5.0 * center)
@@ -513,9 +523,21 @@
 
     lax.fori_loop(0, STEPS // 2, pair, 0)
 
+    def stores(f):
+        return [
+            pltpu.make_async_copy(
+                result.at[t, f, :, pl.ds(HALO, rows), :],
+                out.at[f, :, :, pl.ds(t * LANE, LANE)],
+                out_sem.at[t, f],
+            )
+            for t in range(lane_tiles)
+        ]
+
     def gather(f, carry):
         for k in range(LEVELS):
             collect(f, k, f * LEVELS + k)
+        for c in stores(f):
+            c.start()
         return carry
 
     def collect(f, k, p):
@@ -541,16 +563,9 @@
                     ]
 
     lax.fori_loop(0, FIELDS, gather, 0)
-    stores = [
-        pltpu.make_async_copy(
-            result.at[t, :, :, middle, :], out.at[:, :, :, pl.ds(t * LANE, LANE)], out_sem.at[t]
-        )
-        for t in range(cols // LANE)
-    ]
-    for c in stores:
-        c.start()
-    for c in stores:
-        c.wait()
+    for f in range(FIELDS):
+        for c in stores(f):
+            c.wait()
 
 
 def body(lons, lats, ocean_state, mixing, land_sea):
@@ -605,7 +620,7 @@
             pltpu.VMEM((depth, tiles + 1, SUB, LANE), f32),
             pltpu.VMEM((LEVELS, depth + 2, tiles + 2, SUB, LANE), f32),
             pltpu.VMEM((lane_tiles, FIELDS, LEVELS, ext, LANE), f32),
-            pltpu.SemaphoreType.DMA((lane_tiles,)),
+            pltpu.SemaphoreType.DMA((lane_tiles, FIELDS)),
         ],
         compiler_params=pltpu.CompilerParams(vmem_limit_bytes=32 * 2**20),
         name="substeps",

time: 51.1 us -> 51.4 us (level); the launches traced: 50.9 us -> 50.5 us
    pallas_call x1, Pallas kernels: 32.6 us -> 32 us  [body(): pl.pallas_call(substeps_kernel, out_shape=jax.ShapeDtypeStruct(ocean_stat...]
where the time goes in v4:
time: 51.4 us; the launch traced here: 50.5 us
  Pallas kernels  47.2 us (92%)
  local copies, waits for them, and re-layouts  3.31 us (6%)
    pallas_call x1, Pallas kernels, body(): pl.pallas_call(substeps_kernel, out_shape=jax.ShapeDtypeStruct(ocean_stat...  32 us
    pallas_call x1, Pallas kernels, body(): pl.pallas_call(functools.partial(exchange_kernel, lons, lats), out_shape=...  15.2 us
    unnamed x6, local copies, waits for them, and re-layouts  3.31 us

profile of v4, /device:TPU:7, one launch (start us, length us, event | category | flops | bytes accessed | tf_op | source)
XLA Modules:
  0.0 50.5 jit_solution(12881917546487162763)
XLA Ops:
  0.0 0.0 copy-start
  0.0 1.4 %copy-done = f32[4,3,128,256]{3,2,1,0:T(8,128)S(1)} copy-done((f32[4,3,128,256]{3,2,1,0:T(8,128)S(1)}, f32[4,3,128,256]{3,2,1,0:T(8,128)}, u32[]{:S(2)}) %copy-start) | copy-done | bytes 1572888
  1.4 0.0 copy-start.1
  1.4 1.0 %copy-done.1 = f32[3,128,256]{2,1,0:T(8,128)S(1)} copy-done((f32[3,128,256]{2,1,0:T(8,128)S(1)}, f32[3,128,256]{2,1,0:T(8,128)}, u32[]{:S(2)}) %copy-start.1) | copy-done | bytes 393240
  2.4 0.0 copy-start.2
  2.4 0.9 %copy-done.2 = s32[128,256]{1,0:T(8,128)S(1)} copy-done((s32[128,256]{1,0:T(8,128)S(1)}, s32[128,256]{1,0:T(8,128)}, u32[]{:S(2)}) %copy-start.2) | copy-done | bytes 131096
  3.3 15.2 %exchange.1 = (f32[2,16,160,128]{3,2,1,0:T(8,128)S(1)}, f32[2,160,128]{2,1,0:T(8,128)S(1)}, f32[2,160,128]{2,1,0:T(8,128)S(1)}, bf16[384,384]{1,0:T(8,128)(2,1)S...) custom-call(f32[4,3,128,256]{3,2,1,0:T(8,128)S(1)} %copy-done, f32[3,128,256]{2,1,0:T(8,128)S(1)} %copy-done.1, ...), custom_call_target="tpu_custom_call" | custom-call | tf_op jit(solution)/shard_map/exchange/pallas_call | solution.py:580
  18.5 32.0 %substeps.1 = f32[4,3,128,256]{3,2,1,0:T(8,128)} custom-call(f32[2,16,160,128]{3,2,1,0:T(8,128)S(1)} %get-tuple-element.11.natural, f32[2,160,128]{2,1,0:T(8,128)S(1)} %get-tuple-element.12.west, f32[2,160,128]{2,1,0:T(8,128)S(1)} %get-tuple-element.13.east, bf16[384,384]{1,0:T(8,128)(2,1)S(1)} %get-tuple-element.14.to_tiles, ...), custom_call_target="tpu_custom_call" | custom-call | tf_op jit(solution)/shard_map/substeps/pallas_call | solution.py:609
Async XLA Ops:
  0.0 1.4 %copy-start = (f32[4,3,128,256]{3,2,1,0:T(8,128)S(1)}, f32[4,3,128,256]{3,2,1,0:T(8,128)}, u32[]{:S(2)}) copy-start(f32[4,3,128,256]{3,2,1,0:T(8,128)} %state.1) | copy-start | bytes 4718596
  1.4 1.0 %copy-start.1 = (f32[3,128,256]{2,1,0:T(8,128)S(1)}, f32[3,128,256]{2,1,0:T(8,128)}, u32[]{:S(2)}) copy-start(f32[3,128,256]{2,1,0:T(8,128)} %mixing.1) | copy-start | bytes 1179652
  2.4 0.9 %copy-start.2 = (s32[128,256]{1,0:T(8,128)S(1)}, s32[128,256]{1,0:T(8,128)}, u32[]{:S(2)}) copy-start(s32[128,256]{1,0:T(8,128)} %land.1) | copy-start | bytes 393220

commit v5 on v3

--- a/solution.py
+++ b/solution.py
@@ -234,6 +234,9 @@
     def kept_west():
         return pltpu.make_async_copy(corner_west, west.at[:, high, :], keep_sem.at[1])
 
+    westward().start()
+    eastward().start()
+
     @pl.when(has_south)
     def _():
         for c in southward():
@@ -263,9 +266,6 @@
         @pl.when(across_west == lon)
         def _():
             kept_west().start()
-
-    westward().start()
-    eastward().start()
 
     @pl.when(jnp.logical_not(has_south))
     def _():
@@ -346,8 +346,6 @@
     rows, cols = ext - 2 * HALO, lane_tiles * LANE
     depth = spin.shape[0]
     tiles = mix.shape[2]
-    middle = pl.ds(HALO, rows)
-
     lane = lax.broadcasted_iota(jnp.int32, (SUB, LANE), 1)
     lower_half = lane < HALF
     west_at = tiles * HALF - cols - HALO
@@ -430,9 +428,6 @@
             mix[p, :, c] = value.reshape(depth, SUB, LANE)
     mix[LEVELS] = TIMESTEP * mix[LEVELS]
 
-    def face(before, a, b, after):
-        return 7.0 * (a + b) - (before + after)
-
     def weigh(q):
         for j in range(-1, depth + 1):
             beside = 1 if 0 <= j < depth else 0
@@ -454,10 +449,10 @@
             above, under = jnp.maximum(k - 1, 0), jnp.minimum(k + 1, LEVELS - 1)
             for j in range(depth + 1):
                 for c in each:
-                    fast[j, c] = (q[merid, j + 1, c + edge] + q[merid, j + 2, c + edge]) * (1.0 / 24.0)
+                    fast[j, c] = (q[merid, j + 1, c + edge] + q[merid, j + 2, c + edge]) * (1.0 / 3.0)
             for j in range(depth):
                 for c in range(tiles + 1):
-                    along[j, c] = (q[zonal, j + 2, c + 1] + q[zonal, j + 2, c + 2]) * (1.0 / 24.0)
+                    along[j, c] = (q[zonal, j + 2, c + 1] + q[zonal, j + 2, c + 2]) * (1.0 / 3.0)
             for f in range(FIELDS):
                 p = f * LEVELS + k
 
@@ -465,11 +460,15 @@
                     return [q[p, j + 2, c + edge] for c in each]
 
                 lines = {j: line(j) for j in (-2, -1, 0)}
+                near = {-1: [lines[-2][c] + lines[0][c] for c in each]}
+                bent = {-1: [lines[-1][c] - 0.125 * near[-1][c] for c in each]}
                 lower = None
                 for j in range(-1, depth):
                     lines[j + 2] = line(j + 2)
-                    prev, here, succ, succ2 = (lines[j + d] for d in (-1, 0, 1, 2))
-                    upper = [fast[j + 1, c] * face(prev[c], here[c], succ[c], succ2[c]) for c in each]
+                    here = lines[j]
+                    near[j + 1] = [lines[j][c] + lines[j + 2][c] for c in each]
+                    bent[j + 1] = [lines[j + 1][c] - 0.125 * near[j + 1][c] for c in each]
+                    upper = [fast[j + 1, c] * (bent[j][c] + bent[j + 1][c]) for c in each]
                     if j < 0:
                         lower = upper
                         continue
@@ -478,15 +477,14 @@
                         + here
                         + [q[p, j + 2, tiles + edge], q[p, j + 2, tiles + edge + 1]]
                     )
-                    flux = [
-                        along[j, c] * face(ring[c], ring[c + 1], ring[c + 2], ring[c + 3])
-                        for c in range(tiles + 1)
-                    ]
+                    beside = [ring[c] + ring[c + 2] for c in range(tiles + 2)]
+                    curved = [ring[c + 1] - 0.125 * beside[c] for c in range(tiles + 2)]
+                    flux = [along[j, c] * (curved[c] + curved[c + 1]) for c in range(tiles + 1)]
                     row = []
                     for c in each:
                         center = here[c]
                         advection = (flux[c + 1] - flux[c]) + (upper[c] - lower[c])
-                        around = (ring[c + 1] + ring[c + 3]) + (prev[c] + succ[c])
+                        around = beside[c + 1] + near[j][c]
                         if f < 2:
                             others = q[f * LEVELS + above, j + 2, c + edge] + q[f * LEVELS + under, j + 2, c + edge]
                             mixed = around + (0.5 * others - 5.0 * center)
@@ -513,9 +511,21 @@
 
     lax.fori_loop(0, STEPS // 2, pair, 0)
 
+    def stores(f):
+        return [
+            pltpu.make_async_copy(
+                result.at[t, f, :, pl.ds(HALO, rows), :],
+                out.at[f, :, :, pl.ds(t * LANE, LANE)],
+                out_sem.at[t, f],
+            )
+            for t in range(lane_tiles)
+        ]
+
     def gather(f, carry):
         for k in range(LEVELS):
             collect(f, k, f * LEVELS + k)
+        for c in stores(f):
+            c.start()
         return carry
 
     def collect(f, k, p):
@@ -541,16 +551,9 @@
                     ]
 
     lax.fori_loop(0, FIELDS, gather, 0)
-    stores = [
-        pltpu.make_async_copy(
-            result.at[t, :, :, middle, :], out.at[:, :, :, pl.ds(t * LANE, LANE)], out_sem.at[t]
-        )
-        for t in range(cols // LANE)
-    ]
-    for c in stores:
-        c.start()
-    for c in stores:
-        c.wait()
+    for f in range(FIELDS):
+        for c in stores(f):
+            c.wait()
 
 
 def body(lons, lats, ocean_state, mixing, land_sea):
@@ -605,7 +608,7 @@
             pltpu.VMEM((depth, tiles + 1, SUB, LANE), f32),
             pltpu.VMEM((LEVELS, depth + 2, tiles + 2, SUB, LANE), f32),
             pltpu.VMEM((lane_tiles, FIELDS, LEVELS, ext, LANE), f32),
-            pltpu.SemaphoreType.DMA((lane_tiles,)),
+            pltpu.SemaphoreType.DMA((lane_tiles, FIELDS)),
         ],
         compiler_params=pltpu.CompilerParams(vmem_limit_bytes=32 * 2**20),
         name="substeps",

time: 51.1 us -> 50.8 us (level)
  Pallas kernels: 47.6 us -> 47 us
    pallas_call x1, Pallas kernels: 32.6 us -> 32 us  [body(): pl.pallas_call(substeps_kernel, out_shape=jax.ShapeDtypeStruct(ocean_stat...]
where the time goes in v5:
time: 50.8 us; the launch traced here: 50.3 us
  Pallas kernels  47 us (93%)
  local copies, waits for them, and re-layouts  3.31 us (7%)
    pallas_call x1, Pallas kernels, body(): pl.pallas_call(substeps_kernel, out_shape=jax.ShapeDtypeStruct(ocean_stat...  32 us
    pallas_call x1, Pallas kernels, body(): pl.pallas_call(functools.partial(exchange_kernel, lons, lats), out_shape=...  15 us
    unnamed x6, local copies, waits for them, and re-layouts  3.31 us

profile of v5, /device:TPU:7, one launch (start us, length us, event | category | flops | bytes accessed | tf_op | source)
XLA Modules:
  0.0 50.3 jit_solution(13146122871024691170)
XLA Ops:
  0.0 0.0 copy-start
  0.0 1.4 %copy-done = f32[4,3,128,256]{3,2,1,0:T(8,128)S(1)} copy-done((f32[4,3,128,256]{3,2,1,0:T(8,128)S(1)}, f32[4,3,128,256]{3,2,1,0:T(8,128)}, u32[]{:S(2)}) %copy-start) | copy-done | bytes 1572888
  1.4 0.0 copy-start.1
  1.4 1.0 %copy-done.1 = f32[3,128,256]{2,1,0:T(8,128)S(1)} copy-done((f32[3,128,256]{2,1,0:T(8,128)S(1)}, f32[3,128,256]{2,1,0:T(8,128)}, u32[]{:S(2)}) %copy-start.1) | copy-done | bytes 393240
  2.4 0.0 copy-start.2
  2.4 0.9 %copy-done.2 = s32[128,256]{1,0:T(8,128)S(1)} copy-done((s32[128,256]{1,0:T(8,128)S(1)}, s32[128,256]{1,0:T(8,128)}, u32[]{:S(2)}) %copy-start.2) | copy-done | bytes 131096
  3.3 15.0 %exchange.1 = (f32[2,16,160,128]{3,2,1,0:T(8,128)S(1)}, f32[2,160,128]{2,1,0:T(8,128)S(1)}, f32[2,160,128]{2,1,0:T(8,128)S(1)}, bf16[384,384]{1,0:T(8,128)(2,1)S...) custom-call(f32[4,3,128,256]{3,2,1,0:T(8,128)S(1)} %copy-done, f32[3,128,256]{2,1,0:T(8,128)S(1)} %copy-done.1, ...), custom_call_target="tpu_custom_call" | custom-call | tf_op jit(solution)/shard_map/exchange/pallas_call | solution.py:568
  18.3 32.0 %substeps.1 = f32[4,3,128,256]{3,2,1,0:T(8,128)} custom-call(f32[2,16,160,128]{3,2,1,0:T(8,128)S(1)} %get-tuple-element.11.natural, f32[2,160,128]{2,1,0:T(8,128)S(1)} %get-tuple-element.12.west, f32[2,160,128]{2,1,0:T(8,128)S(1)} %get-tuple-element.13.east, bf16[384,384]{1,0:T(8,128)(2,1)S(1)} %get-tuple-element.14.to_tiles, ...), custom_call_target="tpu_custom_call" | custom-call | tf_op jit(solution)/shard_map/substeps/pallas_call | solution.py:597
Async XLA Ops:
  0.0 1.4 %copy-start = (f32[4,3,128,256]{3,2,1,0:T(8,128)S(1)}, f32[4,3,128,256]{3,2,1,0:T(8,128)}, u32[]{:S(2)}) copy-start(f32[4,3,128,256]{3,2,1,0:T(8,128)} %state.1) | copy-start | bytes 4718596
  1.4 1.0 %copy-start.1 = (f32[3,128,256]{2,1,0:T(8,128)S(1)}, f32[3,128,256]{2,1,0:T(8,128)}, u32[]{:S(2)}) copy-start(f32[3,128,256]{2,1,0:T(8,128)} %mixing.1) | copy-start | bytes 1179652
  2.4 0.9 %copy-start.2 = (s32[128,256]{1,0:T(8,128)S(1)}, s32[128,256]{1,0:T(8,128)}, u32[]{:S(2)}) copy-start(s32[128,256]{1,0:T(8,128)} %land.1) | copy-start | bytes 393220
